TPU v7x, 256 devices: a whole 4x4x8 slice. The times are simulated.
256 devices in a mesh: item: 8 (over z), tensor: 32 (over x, y, core).
Axes of the slice: x: 4, y: 4, z: 8, core: 2. Of those that a mesh axis runs over, the one named last changes fastest.
Arguments:
- gated_hidden_input: bfloat16 [6144, 14336], P('item', 'tensor'), may hold values from -6 to 6
- residual_stream_input: bfloat16 [6144, 8192], P('item', 'tensor'), may hold values from -6 to 6
- down_matrix: bfloat16 [14336, 8192], P('tensor'), may hold values from -0.046875 to 0.046875
- adapter_input_factor: bfloat16 [16, 14336], P(None, 'tensor'), may hold values from -0.046875 to 0.046875
- adapter_output_factor: bfloat16 [16, 8192], P(None, 'tensor'), may hold values from -1.5 to 1.5
- final_norm_scale: bfloat16 [8192], P('tensor'), may hold values from 0.5 to 1.5
- answer_head_rows: bfloat16 [4, 8192], P(None, 'tensor'), may hold values from -0.0625 to 0.0625
- answer_prior_offsets: float32 [6144, 4], P('item'), may hold values from -320 to 320
- input_factor_direction: bfloat16 [2, 16, 14336], P(None, None, 'tensor'), may hold values from -6 to 6
- output_factor_direction: bfloat16 [2, 16, 8192], P(None, None, 'tensor'), may hold values from -1.5 to 1.5
Outputs:
- ggn_a: float32 [2, 16, 14336], P(None, None, 'tensor')
- curvature_output_parts: float32 [2, 16, 8192], P(None, None, 'tensor')
All inputs are finite; a program needn't handle non-finite values.
Results may differ from a plain program's by a relative error of at most 0.0003.
Values may be sent and summed in bfloat16 or wider, within the bound.
A program may use at most 128 MiB of HBM per device.

v0:
```python
import jax
import jax.numpy as jnp
from jax import lax
from jax.sharding import PartitionSpec as P

ADAPTER_SCALE = 2.0
EPS = 1e-05


def class_weights(logits):
    top = jnp.max(logits, axis=1, keepdims=True)
    expo = jnp.exp(logits - top)
    return expo / jnp.sum(expo, axis=1, keepdims=True)


def shards(
    gated_hidden_input,
    residual_stream_input,
    down_matrix,
    adapter_input_factor,
    adapter_output_factor,
    final_norm_scale,
    answer_head_rows,
    answer_prior_offsets,
    input_factor_direction,
    output_factor_direction,
):
    highest_precision = lax.Precision.HIGHEST
    width = lax.axis_size("tensor")
    rows = gated_hidden_input.shape[0]
    feedfwd_piece = gated_hidden_input.shape[1]
    adapter_rank_value = adapter_input_factor.shape[0]
    item_count = input_factor_direction.shape[0]
    model_width = down_matrix.shape[1]
    d_part = model_width // width
    total_rows = rows * lax.axis_size("item")
    column = lax.axis_index("tensor") * d_part
    stacked_parts = jnp.concatenate(
        [adapter_input_factor[None], input_factor_direction], 0
    ).reshape((item_count + 1) * adapter_rank_value, feedfwd_piece)
    lowrank = jnp.dot(gated_hidden_input, stacked_parts.T, preferred_element_type=jnp.float32)
    x_wide = gated_hidden_input.astype(jnp.float32)
    term = jnp.dot(gated_hidden_input, down_matrix, preferred_element_type=jnp.float32)
    res = residual_stream_input.astype(jnp.float32)
    old = lax.dynamic_slice_in_dim(term, column, d_part, 1)
    summed_parts = lax.psum_scatter(
        lax.dynamic_update_slice_in_dim(term, old + res, column, 1),
        "tensor",
        scatter_dimension=1,
        tiled=True,
    )
    ranks = lax.psum(lowrank, "tensor")
    input_times_factor = ranks[:, :adapter_rank_value]
    input_times_direction = (
        ranks[:, adapter_rank_value:]
        .reshape(rows, item_count, adapter_rank_value)
        .transpose(1, 0, 2)
    )
    output_factor = adapter_output_factor.astype(jnp.float32)
    direction_wide_matrix = output_factor_direction.astype(jnp.float32)
    gain = final_norm_scale.astype(jnp.float32)
    head = answer_head_rows.astype(jnp.float32)
    hidden_state = summed_parts + ADAPTER_SCALE * jnp.dot(
        input_times_factor, output_factor, precision=highest_precision
    )
    hidden_delta = ADAPTER_SCALE * (
        jnp.einsum("aqe,eu->aqu", input_times_direction, output_factor, precision=highest_precision)
        + jnp.einsum(
            "gs,ysp->ygp", input_times_factor, direction_wide_matrix, precision=highest_precision
        )
    )
    square_sum, cross_sum = lax.psum(
        (
            jnp.sum(hidden_state * hidden_state, axis=1),
            jnp.sum(hidden_state[None] * hidden_delta, axis=2),
        ),
        "tensor",
    )
    rank_index = lax.rsqrt(square_sum / model_width + EPS)[:, None]
    m = (cross_sum / model_width)[:, :, None]
    normed = hidden_state * rank_index * gain
    dn = gain * (hidden_delta * rank_index - hidden_state * rank_index**3 * m)
    logit_part, dl = lax.psum(
        (
            jnp.dot(normed, head.T, precision=highest_precision),
            jnp.einsum("ktd,cd->ktc", dn, head, precision=highest_precision),
        ),
        "tensor",
    )
    p = class_weights(logit_part + answer_prior_offsets)
    q = p * (dl - jnp.sum(p * dl, axis=2, keepdims=True)) / total_rows
    gbar = gain * jnp.einsum("ktc,cd->ktd", q, head, precision=highest_precision)
    back_sum, mean_gradient_projected, hidden_projected = lax.psum(
        (
            jnp.sum(hidden_state * gbar, axis=2),
            jnp.einsum("mjb,pb->mjp", gbar, output_factor, precision=highest_precision),
            jnp.dot(hidden_state, output_factor.T, precision=highest_precision),
        ),
        "tensor",
    )
    probability_weights = (back_sum / model_width)[:, :, None]
    mean_hidden = rank_index * gbar - hidden_state * rank_index**3 * probability_weights
    output_factor_gradient = ADAPTER_SCALE * jnp.einsum(
        "cf,mce->mfe", input_times_factor, mean_hidden, precision=highest_precision
    )
    direction_output = ADAPTER_SCALE * (
        rank_index * mean_gradient_projected
        - rank_index**3 * probability_weights * hidden_projected
    )
    grad_a = jnp.einsum("ktr,tf->krf", direction_output, x_wide, precision=highest_precision)
    ggn_a, curvature_output_parts = lax.psum((grad_a, output_factor_gradient), "item")
    return (ggn_a, curvature_output_parts)


def solution(mesh):
    placed = (
        P("item", "tensor"),
        P("item", "tensor"),
        P("tensor", None),
        P(None, "tensor"),
        P(None, "tensor"),
        P("tensor"),
        P(None, "tensor"),
        P("item", None),
        P(None, None, "tensor"),
        P(None, None, "tensor"),
    )
    return jax.shard_map(
        shards,
        mesh=mesh,
        in_specs=placed,
        out_specs=(P(None, None, "tensor"), P(None, None, "tensor")),
        check_vma=False,
    )
```

profile of v0, /device:TPU:2, one launch (start us, length us, event | category | flops | bytes accessed | tf_op | source)
XLA Modules:
  0.0 744.0 jit_solution(10948685360716266802)
XLA Ops:
  7.2 0.0 copy-start
  7.2 0.0 all-reduce.8.cloned.1.call-start
  7.2 0.8 pad_maximum_fusion
  8.1 0.2 copy-done
  8.3 0.9 convolution_bitcast_fusion
  9.2 0.0 all-reduce.8.cloned.1.call-update
  9.2 0.0 reduce-scatter.2.cloned.1.call-start
  9.3 0.0 copy-start.3
  9.3 14.9 %fusion.60 = f32[768,8192]{1,0:T(8,128)} fusion(bf16[768,448]{0,1:T(8,128)(2,1)S(1)} %copy-done, bf16[448,8192]{1,0:T(8,128)(2,1)} %param.12), kind=kOutput, calls=%fused_computation.76 | convolution fusion | flops 5637144576 | bytes 33193984 | tf_op jit(solution)/shard_map/dot_general | solution.py:43
  24.2 0.0 copy-done.3
  24.2 2.1 add_dynamic-update-slice_fusion
  26.3 0.0 reduce-scatter.2.cloned.1.call-update
  26.3 0.0 copy-start.4
  26.3 0.0 all-reduce.10.cloned.1.call-start
  26.4 0.6 copy-done.8
  26.9 94.1 %all-reduce.8.cloned.1.call-done = f32[768,48]{0,1:T(8,128)} async-done(((f32[768,48]{0,1:T(8,128)}), f32[768,48]{0,1:T(8,128)}) %all-reduce.8.cloned.1.call-update) | async-done | bytes 147472 | tf_op jit(solution)/shard_map/psum | solution.py:52
  121.0 0.0 copy-done.6
  121.0 2.9 fusion.35
  123.9 149.5 %reduce-scatter.2.cloned.1.call-done = f32[768,256]{1,0:T(8,128)} async-done(((f32[768,8192]{1,0:T(8,128)}), f32[768,256]{1,0:T(8,128)}) %reduce-scatter.2.cloned.1.call-update) | async-done | bytes 786448 | tf_op jit(solution)/shard_map/reduce_scatter | solution.py:46
  273.4 0.0 copy-done.4
  273.4 0.0 copy-done.1
  273.4 1.8 multiply_reduce_fusion.2
  275.2 1.1 copy.16
  276.3 0.5 fusion.61
  276.8 0.3 copy.14
  277.1 0.1 slice-done
  277.2 3.6 multiply_reduce_fusion.1
  280.8 108.6 %all-reduce.2 = (f32[2,768]{1,0:T(2,128)S(1)}, f32[768]{0:T(1024)S(1)}) all-reduce(f32[2,768]{1,0:T(2,128)S(1)} %get-tuple-element.21, f32[768]{0:T(1024)S(1)} %get-tuple-element.12), channel_id=1, replica_groups=mesh['item'=8,'tensor'=32] {'tensor'}, use_global_device_ids=true, to_apply=%region_8.0 | all-reduce | flops 2304 | bytes 18432 | tf_op jit(solution)/shard_map/psum | solution.py:72
  389.4 0.2 broadcast_multiply_fusion
  389.5 0.3 copy.13
  389.8 0.2 copy-done.5
  390.0 0.6 fusion.22
  390.6 2.3 fusion.4
  392.9 123.8 %all-reduce.1 = (f32[2,768,4]{1,2,0:T(4,128)S(1)}, f32[768,4]{0,1:T(4,128)S(1)}) all-reduce(f32[2,768,4]{1,2,0:T(4,128)S(1)} %fusion.4, f32[768,4]{0,1:T(4,128)S(1)} %fusion.22), channel_id=1, replica_groups=mesh['item'=8,'tensor'=32] {'tensor'}, use_global_device_ids=true, to_apply=%region_9.0 | all-reduce | flops 9216 | bytes 73728 | tf_op jit(solution)/shard_map/psum | solution.py:83
  516.7 0.0 copy-done.7
  516.8 0.0 copy-start.2
  516.9 2.1 multiply_reduce_fusion
  519.0 1.3 fusion.52
  520.2 0.0 all-reduce.10.cloned.1.call-update
  520.3 0.0 all-reduce.12.cloned.1.call-start
  520.3 123.8 %all-reduce = (f32[768,16]{0,1:T(8,128)S(1)}, f32[2,768]{1,0:T(2,128)S(1)}) all-reduce(f32[768,16]{0,1:T(8,128)S(1)} %fusion.61, f32[2,768]{1,0:T(2,128)S(1)} %get-tuple-element.23), channel_id=1, replica_groups=mesh['item'=8,'tensor'=32] {'tensor'}, use_global_device_ids=true, to_apply=%region_14.0 | all-reduce | flops 13824 | bytes 110592 | tf_op jit(solution)/shard_map/psum | solution.py:93
  644.1 0.0 copy-done.2
  644.1 2.2 fusion.13
  646.3 2.2 fusion.26
  648.6 0.0 all-reduce.12.cloned.1.call-update
  648.6 86.0 %all-reduce.12.cloned.1.call-done = (f32[2,16,448]{2,1,0:T(8,128)}, f32[2,16,256]{2,1,0:T(8,128)}) async-done(((f32[2,16,448]{2,1,0:T(8,128)}, f32[2,16,256]{2,1,0:T(8,128)}), (f32[2,16,448]{2,1,0:T(8,128)}, f32[2,16,256]{2,1,0:T(8,128)})) %all-reduce.12.cloned.1.call-update) | async-done | bytes 90128 | tf_op jit(solution)/shard_map/psum | solution.py:111
  734.6 1.5 copy.26
  736.1 1.4 copy.27
  (15 shorter events, 0.1 us)
Async XLA Ops:
  7.2 1.1 copy-start
  7.2 113.8 %all-reduce.8.cloned.1.call-start = ((), (), s32[]{:S(2)}) async-start(), calls=%async_computation.2 | async-start | bytes 294912 | tf_op jit(solution)/shard_map/psum | solution.py:52
  9.2 264.2 %reduce-scatter.2.cloned.1.call-start = ((), (), s32[]{:S(2)}) async-start(), calls=%async_computation.1 | async-start | bytes 25952256 | tf_op jit(solution)/shard_map/reduce_scatter | solution.py:46
  9.3 14.9 %copy-start.3 = (bf16[768,256]{1,0:T(8,128)(2,1)S(1)}, bf16[768,256]{1,0:T(8,128)(2,1)}, u32[]{:S(2)}) copy-start(bf16[768,256]{1,0:T(8,128)(2,1)} %param.11) | copy-start | bytes 1179652
  26.3 0.7 copy-start.8
  26.3 94.7 %copy-start.6 = (bf16[2,16,256]{2,1,0:T(8,128)(2,1)S(1)}, bf16[2,16,256]{2,1,0:T(8,128)(2,1)}, u32[]{:S(2)}) copy-start(bf16[2,16,256]{2,1,0:T(8,128)(2,1)} %param.19) | copy-start | bytes 49156
  26.3 247.1 %copy-start.4 = (bf16[16,256]{1,0:T(8,128)(2,1)S(1)}, bf16[16,256]{1,0:T(8,128)(2,1)}, u32[]{:S(2)}) copy-start(bf16[16,256]{1,0:T(8,128)(2,1)} %param.14) | copy-start | bytes 24580
  26.3 620.0 %all-reduce.10.cloned.1.call-start = ((), (), s32[]{:S(2)}) async-start(), calls=%async_computation.3 | async-start | bytes 196608 | tf_op jit(solution)/shard_map/psum | solution.py:93
  121.0 152.4 %copy-start.1 = (f32[768,48]{0,1:T(8,128)S(1)}, f32[768,48]{0,1:T(8,128)}, u32[]{:S(2)}) copy-start(f32[768,48]{0,1:T(8,128)} %all-reduce.8.cloned.1.call-done) | copy-start | bytes 442372
  276.3 0.9 slice-start
  389.4 0.7 copy-start.5
  390.0 126.7 %copy-start.7 = (f32[768,4]{0,1:T(4,128)S(1)}, f32[768,4]{0,1:T(4,128)}, u32[]{:S(2)}) copy-start(f32[768,4]{0,1:T(4,128)} %param.17) | copy-start | bytes 36868
  516.8 127.3 %copy-start.2 = (f32[768,48]{0,1:T(8,128)S(1)}, f32[768,48]{0,1:T(8,128)}, u32[]{:S(2)}) copy-start(f32[768,48]{0,1:T(8,128)} %all-reduce.8.cloned.1.call-done) | copy-start | bytes 442372
  520.3 214.3 %all-reduce.12.cloned.1.call-start = ((), (), s32[]{:S(2)}) async-start(), calls=%async_computation.4 | async-start | bytes 196608 | tf_op jit(solution)/shard_map/psum | solution.py:111
Sparse Core Ops, SparseCore 0:
  11.3 109.6 all-reduce.7
  125.8 147.5 reduce-scatter.1
  520.4 122.0 all-reduce.9
  648.7 85.8 all-reduce.11
where the time goes:
time: 745 us; the launch traced here: 744 us
  blocking collectives  356 us (48%)
  waiting for transfers between devices  330 us (44%)
  matrix products  35.2 us (5%)
  between operations  13.9 us (2%)
    reduce_scatter x1, waiting for transfers between devices, shards(): lax.psum_scatter(lax.dynamic_update_slice_in_dim(term, old + res, column,...  149 us
    psum x1, blocking collectives, shards(): lax.psum((jnp.sum(hidden_state * gbar, axis=2), jnp.einsum('mjb,pb->mjp',...  124 us
    psum x1, blocking collectives, shards(): lax.psum((jnp.dot(normed, head.T, precision=highest_precision), jnp.einsu...  124 us
    psum x1, blocking collectives, shards(): lax.psum((jnp.sum(hidden_state * hidden_state, axis=1), jnp.sum(hidden_st...  109 us
    psum x1, waiting for transfers between devices, shards(): ranks = lax.psum(lowrank, 'tensor')  94.1 us
    psum x1, waiting for transfers between devices, shards(): lax.psum((grad_a, output_factor_gradient), 'item')  86 us
  transfers between devices with their start and end apart: 4, of which 3 were waited for; matrix products, arithmetic and copies ran while one was open for 3% of the time, Pallas kernels for 0%

commit v1 on v0

v1 whole, which is shorter than its diff:
```python
import jax
import jax.numpy as jnp
from jax import lax
from jax.sharding import PartitionSpec as P

SCALE = 2.0
EPS = 1e-05
HI = lax.Precision.HIGHEST


def split3(v):
    a = lax.reduce_precision(v, 8, 7)
    b = lax.reduce_precision(v - a, 8, 7)
    c = v - a - b
    return tuple(part.astype(jnp.bfloat16) for part in (a, b, c))


def shards(x, res, w, a_in, b_out, gain, head, prior, v_in, d_out):
    f32 = jnp.float32
    width = lax.axis_size("tensor")
    rows, piece = x.shape
    rank = a_in.shape[0]
    k = v_in.shape[0]
    model = w.shape[1]
    total_rows = rows * lax.axis_size("item")
    gh = gain.astype(f32)[None] * head.astype(f32)
    g_hi, g_lo, _ = split3(gh)
    classes = head.shape[0]
    proj = jnp.concatenate([b_out, d_out.reshape(k * rank, -1), g_hi, g_lo], 0)
    full = lax.all_gather(proj, "tensor", axis=1, tiled=True)
    y = lax.dot_general(w, full, (((1,), (1,)), ((), ())), preferred_element_type=f32)
    gram = lax.dot_general(full, full, (((1,), (1,)), ((), ())), preferred_element_type=f32)
    av = jnp.concatenate([a_in[None], v_in], 0).reshape((k + 1) * rank, piece)
    low = lax.dot_general(x, av, (((1,), (1,)), ((), ())), preferred_element_type=f32)
    hp = lax.dot_general(res, proj, (((1,), (1,)), ((), ())), preferred_element_type=f32)
    for part in split3(y):
        hp = hp + jnp.dot(x, part, preferred_element_type=f32)
    low = lax.psum(jnp.concatenate([low, hp], 1), "tensor")
    term = jnp.dot(x, w, preferred_element_type=f32).astype(jnp.bfloat16)
    summed = lax.psum_scatter(term, "tensor", scatter_dimension=1, tiled=True).astype(f32)

    xa = low[:, :rank]
    xv = [low[:, rank * (i + 1):rank * (i + 2)] for i in range(k)]
    hp = low[:, rank * (k + 1):] + SCALE * jnp.dot(xa, gram[:rank], precision=HI)
    n = rank * (k + 1)

    def fold(m):
        return jnp.concatenate([m[..., :n], m[..., n:n + classes] + m[..., n + classes:]], -1)

    hp = fold(hp)
    gram = fold(fold(gram).T).T
    h = summed + res.astype(f32) + SCALE * jnp.dot(xa, b_out.astype(f32), precision=HI)
    sq = lax.psum(jnp.sum(h * h, 1), "tensor")
    r = lax.rsqrt(sq / model + EPS)[:, None]
    hg = hp[:, n:]
    hb = hp[:, :rank]
    logits = r * hg + prior
    top = jnp.max(logits, axis=1, keepdims=True)
    ex = jnp.exp(logits - top)
    p = ex / jnp.sum(ex, axis=1, keepdims=True)
    us, cs, qs = [], [], []
    for i in range(k):
        lo, hi_ = rank * (i + 1), rank * (i + 2)
        m = SCALE * jnp.sum(xv[i] * hb + xa * hp[:, lo:hi_], 1, keepdims=True) / model
        dhg = SCALE * (jnp.dot(xv[i], gram[:rank, n:], precision=HI) + jnp.dot(xa, gram[lo:hi_, n:], precision=HI))
        dl = r * dhg - r**3 * m * hg
        q = p * (dl - jnp.sum(p * dl, 1, keepdims=True)) / total_rows
        s = jnp.sum(q * hg, 1, keepdims=True) / model
        us.append(SCALE * (r * jnp.dot(q, gram[n:, :rank], precision=HI) - r**3 * s * hb))
        cs.append(r**3 * s * xa)
        qs.append(r * q)
    u = jnp.concatenate(us, 1)
    c = jnp.concatenate(cs, 1)
    q = jnp.concatenate(qs, 1)
    ggn = 0.0
    for part in split3(u):
        ggn = ggn + lax.dot_general(part, x, (((0,), (0,)), ((), ())), preferred_element_type=f32)
    t1 = lax.dot_general(q, xa, (((0,), (0,)), ((), ())), precision=HI).reshape(k, classes, rank)
    curv = SCALE * (
        jnp.einsum("kce,cd->ked", t1, gh, precision=HI).reshape(k * rank, -1)
        - lax.dot_general(c, h, (((0,), (0,)), ((), ())), precision=HI)
    )
    out = lax.psum(jnp.concatenate([ggn, curv], 1), "item")
    return out[:, :piece].reshape(k, rank, piece), out[:, piece:].reshape(k, rank, -1)


def solution(mesh):
    placed = (
        P("item", "tensor"),
        P("item", "tensor"),
        P("tensor", None),
        P(None, "tensor"),
        P(None, "tensor"),
        P("tensor"),
        P(None, "tensor"),
        P("item", None),
        P(None, None, "tensor"),
        P(None, None, "tensor"),
    )
    return jax.shard_map(
        shards,
        mesh=mesh,
        in_specs=placed,
        out_specs=(P(None, None, "tensor"), P(None, None, "tensor")),
        check_vma=False,
    )
```

time: 745 us -> 422 us (0.57)
  blocking collectives: 356 us -> 79.7 us
  waiting for transfers between devices: 330 us -> 288 us
    psum x3 -> x1, blocking collectives: 356 us -> 54.1 us  [shards(): sq = lax.psum(jnp.sum(h * h, 1), 'tensor')]
    reduce_scatter x1, waiting for transfers between devices: 149 us -> 111 us  [shards(): lax.psum_scatter(term, 'tensor', scatter_dimension=1, tiled=True)]
    all_gather x0 -> x1, blocking collectives: none -> 25.6 us  [shards(): full = lax.all_gather(proj, 'tensor', axis=1, tiled=True)]
    dot_general x12 -> x22, matrix products: 35.2 us -> 30.6 us  [the longest x1 12.7 us: shards(): term = jnp.dot(x, w, preferred_element_type=f32).astype(jnp.bfloat16)]
    psum x3 -> x2, waiting for transfers between devices: 180 us -> 177 us  [the longest x1 98.7 us: shards(): low = lax.psum(jnp.concatenate([low, hp], 1), 'tensor')]
  transfers between devices with their start and end apart: 4 -> 3, of which waited for: 3 -> 3; matrix products, arithmetic and copies ran while one was open for 3% -> 4% of each run, Pallas kernels for 0% -> 0%
where the time goes in v1:
time: 422 us; the launch traced here: 421 us
  waiting for transfers between devices  288 us (68%)
  blocking collectives  79.7 us (19%)
  matrix products  30.6 us (7%)
  between operations  14 us (3%)
  other arithmetic  5.61 us (1%)
    reduce_scatter x1, waiting for transfers between devices, shards(): lax.psum_scatter(term, 'tensor', scatter_dimension=1, tiled=True)  111 us
    psum x1, waiting for transfers between devices, shards(): low = lax.psum(jnp.concatenate([low, hp], 1), 'tensor')  98.7 us
    psum x1, waiting for transfers between devices, shards(): out = lax.psum(jnp.concatenate([ggn, curv], 1), 'item')  78.3 us
    psum x1, blocking collectives, shards(): sq = lax.psum(jnp.sum(h * h, 1), 'tensor')  54.1 us
    all_gather x1, blocking collectives, shards(): full = lax.all_gather(proj, 'tensor', axis=1, tiled=True)  25.6 us
    dot_general x1, matrix products, shards(): term = jnp.dot(x, w, preferred_element_type=f32).astype(jnp.bfloat16)  12.7 us
  transfers between devices with their start and end apart: 3, of which 3 were waited for; matrix products, arithmetic and copies ran while one was open for 4% of the time, Pallas kernels for 0%

profile of v1, /device:TPU:2, one launch (start us, length us, event | category | flops | bytes accessed | tf_op | source)
XLA Modules:
  0.0 421.4 jit_solution(1066382299249914560)
XLA Ops:
  7.2 0.0 copy-start
  7.2 0.0 copy-start.4
  7.2 0.0 copy-start.3
  7.2 0.0 all-reduce.3.cloned.1.call-start
  7.2 0.7 convert_element_type.43
  8.0 0.7 reduce-precision_convert_fusion.8
  8.6 0.7 pad_maximum_fusion.4
  9.4 25.6 %all_gather.3 = bf16[56,8192]{1,0:T(8,128)(2,1)S(1)} all-gather(bf16[56,256]{1,0:T(8,128)(2,1)S(1)} %pad_maximum_fusion.4), channel_id=1, replica_groups=mesh['item'=8,'tensor'=32] {'tensor'}, dimensions={1}, use_global_device_ids=true | all-gather | bytes 946176 | tf_op jit(solution)/shard_map/all_gather | solution.py:30
  35.0 1.3 fusion.61
  36.3 5.3 %convolution_bitcast_fusion.1 = f32[448,56]{0,1:T(8,128)S(1)} fusion(bf16[56,8192]{1,0:T(8,128)(2,1)S(1)} %all_gather.3, bf16[448,8192]{1,0:T(8,128)(2,1)} %param.12), kind=kOutput, calls=%fused_computation.10 | convolution fusion | flops 411041792 | bytes 8357888 | tf_op jit(solution)/shard_map/dot_general | solution.py:31
  41.6 0.2 convolution_add_fusion.2
  41.8 0.2 convolution_add_fusion.1
  42.1 0.2 fusion.1
  42.3 0.2 convolution_bitcast_fusion
  42.6 0.8 pad_maximum_fusion
  43.3 0.0 all-reduce.3.cloned.1.call-update
  43.4 0.0 reduce-scatter.2.cloned.1.call-start
  43.4 12.7 %convolution_convert_fusion = bf16[768,8192]{1,0:T(8,128)(2,1)} fusion(bf16[768,448]{0,1:T(8,128)(2,1)S(1)} %copy-done, bf16[448,8192]{1,0:T(8,128)(2,1)} %param.12), kind=kOutput, calls=%fused_computation | convolution fusion | flops 5643436032 | bytes 20611072 | tf_op jit(solution)/shard_map/dot_general | solution.py:39
  56.2 0.0 reduce-scatter.2.cloned.1.call-update
  56.2 0.0 all-reduce.5.cloned.1.call-start
  56.2 0.4 fusion.64
  56.7 0.1 slice_add_fusion
  56.8 0.1 maximum_bitcast_fusion.1
  56.8 98.7 %all-reduce.3.cloned.1.call-done = f32[768,104]{0,1:T(8,128)} async-done(((f32[768,104]{0,1:T(8,128)}), f32[768,104]{0,1:T(8,128)}) %all-reduce.3.cloned.1.call-update) | async-done | bytes 319504 | tf_op jit(solution)/shard_map/psum | solution.py:38
  155.6 1.2 fusion.2
  156.8 0.9 fusion.23
  157.7 1.0 fusion.24
  158.7 1.0 fusion.26
  159.6 111.2 %reduce-scatter.2.cloned.1.call-done = bf16[768,256]{1,0:T(8,128)(2,1)} async-done(((bf16[768,8192]{1,0:T(8,128)(2,1)}), bf16[768,256]{1,0:T(8,128)(2,1)}) %reduce-scatter.2.cloned.1.call-update) | async-done | bytes 393232 | tf_op jit(solution)/shard_map/reduce_scatter | solution.py:40
  270.9 1.7 multiply_reduce_fusion
  272.5 54.1 %psum.22 = f32[768]{0:T(1024)S(1)} all-reduce(f32[768]{0:T(1024)S(1)} %get-tuple-element.27), channel_id=1, replica_groups=mesh['item'=8,'tensor'=32] {'tensor'}, use_global_device_ids=true, to_apply=%region_3.0 | all-reduce | flops 768 | bytes 6144 | tf_op jit(solution)/shard_map/psum | solution.py:53
  326.7 1.0 fusion.9
  327.7 1.0 multiply_reduce_fusion.4
  328.8 0.2 fusion.6
  329.1 0.2 fusion.4
  329.3 0.3 fusion.19
  329.6 0.3 convolution_add_fusion.4
  329.9 0.3 convolution_add_fusion.3
  330.3 0.9 fusion.29
  331.2 0.1 dot_general.97
  331.4 0.2 fusion.48
  331.6 0.8 slice_multiply_fusion.3
  332.4 0.5 fusion.7
  332.9 0.7 pad_maximum_fusion.2
  333.6 0.0 all-reduce.5.cloned.1.call-update
  333.6 78.3 %all-reduce.5.cloned.1.call-done = f32[32,704]{1,0:T(8,128)} async-done(((f32[32,704]{1,0:T(8,128)}), f32[32,704]{1,0:T(8,128)}) %all-reduce.5.cloned.1.call-update) | async-done | bytes 90128 | tf_op jit(solution)/shard_map/psum | solution.py:83
  412.0 1.5 slice.114
  413.4 1.5 slice.115
  (22 shorter events, 0.2 us)
Async XLA Ops:
  7.2 34.4 %copy-start = (bf16[768,448]{0,1:T(8,128)(2,1)S(1)}, bf16[768,448]{0,1:T(8,128)(2,1)}, u32[]{:S(2)}) copy-start(bf16[768,448]{0,1:T(8,128)(2,1)} %param.10) | copy-start | bytes 2064388
  7.2 35.1 %copy-start.4 = (bf16[16,448]{1,0:T(8,128)(2,1)S(1)}, bf16[16,448]{1,0:T(8,128)(2,1)}, u32[]{:S(2)}) copy-start(bf16[16,448]{1,0:T(8,128)(2,1)} %param.13) | copy-start | bytes 43012
  7.2 35.1 %copy-start.3 = (bf16[2,16,448]{2,1,0:T(8,128)(2,1)S(1)}, bf16[2,16,448]{2,1,0:T(8,128)(2,1)}, u32[]{:S(2)}) copy-start(bf16[2,16,448]{2,1,0:T(8,128)(2,1)} %param.18) | copy-start | bytes 86020
  7.2 148.4 %all-reduce.3.cloned.1.call-start = ((), (), s32[]{:S(2)}) async-start(), calls=%async_computation.2 | async-start | bytes 638976 | tf_op jit(solution)/shard_map/psum | solution.py:38
  43.4 227.5 %reduce-scatter.2.cloned.1.call-start = ((), (), s32[]{:S(2)}) async-start(), calls=%async_computation.1 | async-start | bytes 12976128 | tf_op jit(solution)/shard_map/reduce_scatter | solution.py:40
  56.1 214.7 %copy-start.1 = (bf16[768,256]{1,0:T(8,128)(2,1)S(1)}, bf16[768,256]{1,0:T(8,128)(2,1)}, u32[]{:S(2)}) copy-start(bf16[768,256]{1,0:T(8,128)(2,1)} %param.11) | copy-start | bytes 1179652
  56.1 214.7 %copy-start.2 = (bf16[16,256]{1,0:T(8,128)(2,1)S(1)}, bf16[16,256]{1,0:T(8,128)(2,1)}, u32[]{:S(2)}) copy-start(bf16[16,256]{1,0:T(8,128)(2,1)} %param.14) | copy-start | bytes 24580
  56.1 270.5 %copy-start.5 = (f32[768,4]{0,1:T(4,128)S(1)}, f32[768,4]{0,1:T(4,128)}, u32[]{:S(2)}) copy-start(f32[768,4]{0,1:T(4,128)} %param.17) | copy-start | bytes 36868
  56.1 275.2 %copy-start.6 = (bf16[4,256]{1,0:T(4,128)(2,1)S(1)}, bf16[4,256]{1,0:T(4,128)(2,1)}, u32[]{:S(2)}) copy-start(bf16[4,256]{1,0:T(4,128)(2,1)} %param.16) | copy-start | bytes 6148
  56.2 355.8 %all-reduce.5.cloned.1.call-start = ((), (), s32[]{:S(2)}) async-start(), calls=%async_computation.3 | async-start | bytes 196608 | tf_op jit(solution)/shard_map/psum | solution.py:83
Sparse Core Ops, SparseCore 0:
  43.5 112.0 all-reduce.2
  159.7 111.1 reduce-scatter.1
  333.8 78.1 all-reduce.4

commit v2 on v1

v2 whole, which is shorter than its diff:
```python
import functools

import jax
import jax.numpy as jnp
from jax import lax
from jax.experimental import pallas as pl
from jax.experimental.pallas import tpu as pltpu
from jax.sharding import PartitionSpec as P

SCALE = 2.0
EPS = 1e-05
HI = lax.Precision.HIGHEST
F32 = jnp.float32
BF16 = jnp.bfloat16
N = 4
NT = (((1,), (1,)), ((), ()))
NN = (((1,), (0,)), ((), ()))


def dot(a, b, dims=NN, precision=None):
    return lax.dot_general(a, b, dims, preferred_element_type=F32, precision=precision)


def split3(v):
    a = v.astype(BF16)
    rest = v - a.astype(F32)
    b = rest.astype(BF16)
    c = (rest - b.astype(F32)).astype(BF16)
    return a, b, c


def wrap(v):
    return lax.rem(v, N)


def kernel(
    chunks, zs, total_tokens,
    x_hbm, r_hbm, w_hbm, a_ref, b_ref, g_ref, head_ref, prior_ref, v_ref, d_ref,
    ggn_ref, curv_ref,
    xbuf, rbuf, wbuf, tb, r1, r2, pf, g8, avp, ybuf, gram, lbuf, la, lc, lx, ly, lfull,
    hhi, hlo, ssend, sx, sy, sc, zpart, zrecv, zfull,
    wl, xl, rl, ws, wr, xs, xr, ms, mr, ns, nr, c1s, c1r, c2s, c2r, c3s, c3r, zss, zsr,
):
    rows, piece = x_hbm.shape
    half = rows // 2
    tc = half // chunks
    fb = r_hbm.shape[1]
    lanes = 128
    model = w_hbm.shape[1]
    rank = a_ref.shape[0]
    zi = lax.axis_index("item")
    me = lax.axis_index("tensor")
    core = lax.rem(me, 2)
    chip = lax.div(me, 2)
    px = lax.div(chip, N)
    py = lax.rem(chip, N)

    def device(x, y, c):
        return {"tensor": (x * N + y) * 2 + c}

    sibling = device(px, py, 1 - core)
    xpeer = [None] + [device(wrap(px + o), py, core) for o in range(1, N)]
    ypeer = [None] + [device(px, wrap(py + o), core) for o in range(1, N)]
    zpeer = [None] + [{"item": lax.rem(zi + o, zs)} for o in range(1, zs)]
    sends = []

    def send(src, dst, ssem, rsem, to):
        copy = pltpu.make_async_remote_copy(
            src_ref=src, dst_ref=dst, send_sem=ssem, recv_sem=rsem,
            device_id=to, device_id_type=pl.DeviceIdType.MESH,
        )
        copy.start()
        sends.append(copy)
        return copy

    order = [(2, o) for o in range(N)] + [(o, 2) for o in (0, 1, 3)]
    order += [(i, j) for i in (1, 3, 0) for j in (1, 3, 0)]

    def block(n):
        return wrap(px + order[n][0]) * N + wrap(py + order[n][1])

    def columns(b, c):
        return pl.ds(pl.multiple_of((b * 2 + c) * fb, fb), fb)

    xloads = [
        pltpu.make_async_copy(x_hbm.at[pl.ds(f * half, half)], xbuf.at[0, pl.ds(f * half, half)], xl.at[f])
        for f in range(2)
    ]
    wloads = [
        pltpu.make_async_copy(w_hbm.at[:, columns(block(n), core)], wbuf.at[0, block(n)], wl.at[n])
        for n in range(N * N)
    ]
    rload = pltpu.make_async_copy(r_hbm, rbuf, rl.at[0])
    xloads[0].start()
    for n in range(N):
        wloads[n].start()
    xloads[1].start()
    for n in range(N, N * N):
        wloads[n].start()
    rload.start()

    g8[...] = jnp.zeros_like(g8)
    g8[0:4, :] = head_ref[...].astype(F32) * g_ref[...].astype(F32)
    ghi = g8[...].astype(BF16).astype(F32)
    pf[:, :, 64:128, :] = jnp.zeros((N, N, 64, fb), BF16)
    pf[py, px, 0:rank, :] = b_ref[...]
    pf[py, px, rank:3 * rank, :] = d_ref[...]
    pf[py, px, 3 * rank:64, :] = jnp.concatenate([ghi, g8[...] - ghi], 0).astype(BF16)
    avp[...] = jnp.zeros_like(avp)
    avp[64:64 + rank, :] = a_ref[...]
    avp[64 + rank:64 + 3 * rank, :] = v_ref[...]

    barrier = pltpu.get_barrier_semaphore()
    peers = [sibling] + xpeer[1:] + ypeer[1:] + zpeer[1:]
    for to in peers:
        pl.semaphore_signal(barrier, inc=1, device_id=to, device_id_type=pl.DeviceIdType.MESH)
    pl.semaphore_wait(barrier, len(peers))

    def send_x(f):
        return send(x_hbm.at[pl.ds(f * half, half)], xbuf.at[1, pl.ds(f * half, half)], xs.at[f], xr.at[f], sibling)

    def send_w(n):
        return send(w_hbm.at[:, columns(block(n), 1 - core)], wbuf.at[1, block(n)], ws.at[n], wr.at[n], sibling)

    xin = [send_x(0)]
    win = [send_w(n) for n in range(N)]
    pin = [
        send(pf.at[py, px, pl.ds(0, 64)], pf.at[py, px, pl.ds(0, 64)], c1s.at[0, o - 1], c1r.at[0, o - 1], xpeer[o])
        for o in range(1, N)
    ]
    xin.append(send_x(1))
    win += [send_w(n) for n in range(N, N * N)]

    def recv_slot(src_shape_ref, sem):
        return pltpu.make_async_copy(src_shape_ref, src_shape_ref, sem)

    pos = [(px, py), (py, px)]

    def group(f, i1):
        def body(i2, carry):
            b = i1 * N + i2 if f == 0 else i2 * N + i1
            acc = dot(xbuf[0, f * half:(f + 1) * half, :], wbuf[0, b])
            acc = acc + dot(xbuf[1, f * half:(f + 1) * half, :], wbuf[1, b])
            out = acc.astype(BF16)
            tb[f, i1 * N + i2, 0] = out[:, :lanes]
            tb[f, i1 * N + i2, 1] = out[:, lanes:]
            return carry

        lax.fori_loop(0, N, body, 0)

    def step1(f, o):
        p1 = wrap(pos[f][0] + o)
        peer = xpeer if f == 0 else ypeer
        return p1, peer

    def send_m(f, c, direction, msg):
        peer = xpeer if f == 0 else ypeer
        to = peer[1] if direction == 0 else peer[N - 1]
        offset = 2 if msg == 0 else (1 if direction == 0 else N - 1)
        i1 = wrap(pos[f][0] + offset)
        part = 1 - direction if msg == 1 else direction
        send(
            tb.at[f, pl.ds(i1 * N + 2 * part, 2), :, pl.ds(c * tc, tc), :],
            r1.at[f, c, direction, msg],
            ms.at[f, c, direction, msg], mr.at[f, c, direction, msg], to,
        )

    def wait_m(f, c, direction, msg):
        recv_slot(r1.at[f, c, direction, msg], mr.at[f, c, direction, msg]).wait()

    def send_n(f, c, direction, msg):
        peer = ypeer if f == 0 else xpeer
        to = peer[1] if direction == 0 else peer[N - 1]
        offset = 2 if msg == 0 else (1 if direction == 0 else N - 1)
        i2 = wrap(pos[f][1] + offset)
        part = 1 - direction if msg == 1 else direction
        send(
            tb.at[f, pos[f][0] * N + i2, part, pl.ds(c * tc, tc), :],
            r2.at[f, c, direction, msg],
            ns.at[f, c, direction, msg], nr.at[f, c, direction, msg], to,
        )

    def wait_n(f, c, direction, msg):
        recv_slot(r2.at[f, c, direction, msg], nr.at[f, c, direction, msg]).wait()

    def wait_w(n):
        wloads[n].wait()
        win[n].wait_recv()

    xloads[0].wait()
    xin[0].wait_recv()
    for n in range(N):
        wait_w(n)
    group(0, wrap(px + 2))
    for c in range(chunks):
        for direction in range(2):
            send_m(0, c, direction, 0)
    for copy in pin:
        copy.wait_recv()
    pin2 = [
        send(pf.at[py, :, pl.ds(0, 64)], pf.at[py, :, pl.ds(0, 64)], c1s.at[1, o - 1], c1r.at[1, o - 1], ypeer[o])
        for o in range(1, N)
    ]
    xloads[1].wait()
    xin[1].wait_recv()
    for n in range(N, 2 * N - 1):
        wait_w(n)
    group(1, wrap(py + 2))
    for c in range(chunks):
        for direction in range(2):
            send_m(1, c, direction, 0)
    for n in range(2 * N - 1, N * N):
        wait_w(n)
    for f in range(2):
        group(f, wrap(pos[f][0] + 1))
        group(f, wrap(pos[f][0] + N - 1))
        for c in range(chunks):
            for direction in range(2):
                send_m(f, c, direction, 1)

    def middle(f, c):
        for direction in range(2):
            wait_m(f, c, direction, 0)
            i1 = wrap(pos[f][0] + (1 if direction == 0 else N - 1))
            at = (f, pl.ds(i1 * N + 2 * direction, 2), slice(None), pl.ds(c * tc, tc), slice(None))
            tb[at] = (tb[at].astype(F32) + r1[f, c, direction, 0].astype(F32)).astype(BF16)
            send_m(f, c, direction, 2)

    for f in range(2):
        group(f, pos[f][0])
    for c in range(chunks):
        for f in range(2):
            middle(f, c)

    for copy in pin2:
        copy.wait_recv()
    eye = (
        lax.broadcasted_iota(jnp.int32, (piece, piece), 0) == lax.broadcasted_iota(jnp.int32, (piece, piece), 1)
    ).astype(F32).astype(BF16)
    ybuf[0] = dot(eye, avp[...], NT)
    ybuf[1] = jnp.zeros((piece, lanes), F32)
    gram[0] = jnp.zeros((64, lanes), F32)

    def project(b, carry):
        i, j = lax.div(b, N), lax.rem(b, N)
        p = pf[j, i]
        ybuf[0] = ybuf[0] + dot(wbuf[0, b], p, NT)
        ybuf[1] = ybuf[1] + dot(wbuf[1, b], p, NT)
        gram[0] = gram[0] + dot(p[0:64], p, NT)
        return carry

    lax.fori_loop(0, N * N, project, 0)
    rload.wait()
    for s in range(2):
        for i, part in enumerate(split3(ybuf[s])):
            yi = part
            for f in range(2):
                at = slice(f * half, (f + 1) * half)
                add = dot(xbuf[s, at, :], yi)
                if s == 0 and i == 0:
                    lbuf[at, :] = dot(rbuf[at, :], pf[py, px], NT) + add
                else:
                    lbuf[at, :] = lbuf[at, :] + add
    other = pl.multiple_of((1 - core) * half, half)
    mine = pl.multiple_of(core * half, half)
    lin = send(lbuf.at[pl.ds(other, half)], la, c2s.at[0], c2r.at[0], sibling)
    gin = send(gram.at[0], gram.at[1], c2s.at[1], c2r.at[1], sibling)

    def stage2(f, c):
        wait_m(f, c, 0, 1)
        wait_m(f, c, 1, 1)
        wait_m(f, c, 0, 2)
        wait_m(f, c, 1, 2)
        for part in range(2):
            at = (f, pl.ds(pos[f][0] * N + 2 * part, 2), slice(None), pl.ds(c * tc, tc), slice(None))
            tb[at] = (
                tb[at].astype(F32)
                + r1[f, c, part, 2].astype(F32)
                + r1[f, c, 1 - part, 1].astype(F32)
            ).astype(BF16)
        for msg in range(2):
            for direction in range(2):
                send_n(f, c, direction, msg)

    def stage3(f, c):
        for direction in range(2):
            wait_n(f, c, direction, 0)
            i2 = wrap(pos[f][1] + (1 if direction == 0 else N - 1))
            at = (f, pos[f][0] * N + i2, direction, pl.ds(c * tc, tc), slice(None))
            tb[at] = (tb[at].astype(F32) + r2[f, c, direction, 0].astype(F32)).astype(BF16)
            send_n(f, c, direction, 2)

    lin.wait_recv()
    lc[...] = lbuf[pl.ds(mine, half), :] + la[...]
    q1, q2 = half // N, half // N // N

    def xslice(o):
        return pl.ds(pl.multiple_of(wrap(px + o) * q1, q1), q1)

    bins = [send(lc.at[xslice(o)], lx.at[o - 1], c2s.at[1 + o], c2r.at[1 + o], xpeer[o]) for o in range(1, N)]
    for f in range(2):
        stage2(f, 0)
    for copy in bins:
        copy.wait_recv()
    lc[xslice(0), :] = lc[xslice(0), :] + lx[0] + lx[1] + lx[2]

    def yslice(o):
        return pl.ds(pl.multiple_of(px * q1 + wrap(py + o) * q2, q2), q2)

    cins = [send(lc.at[yslice(o)], ly.at[o - 1], c2s.at[4 + o], c2r.at[4 + o], ypeer[o]) for o in range(1, N)]
    for f in range(2):
        stage3(f, 0)
        stage2(f, 1)
    for copy in cins:
        copy.wait_recv()
    lfull[core, px, py] = lc[yslice(0), :] + ly[0] + ly[1] + ly[2]
    own = lfull.at[core, px, py]
    dins = [send(own, own, c2s.at[7 + o], c2r.at[7 + o], ypeer[o]) for o in range(1, N)]
    for f in range(2):
        stage3(f, 1)
    for copy in dins:
        copy.wait_recv()
    own = lfull.at[core, px]
    eins = [send(own, own, c2s.at[10 + o], c2r.at[10 + o], xpeer[o]) for o in range(1, N)]
    for f in range(2):
        stage2(f, 2)
    for copy in eins:
        copy.wait_recv()
    own = lfull.at[core]
    fin = send(own, own, c2s.at[14], c2r.at[14], sibling)
    for f in range(2):
        stage3(f, 2)
    fin.wait_recv()
    gin.wait_recv()

    low = lfull[...].reshape(rows, lanes)
    lt = low.T
    gm = (gram[0] + gram[1])[:, 0:64]
    xa = lt[64:64 + rank]
    xv = [lt[64 + rank * (i + 1):64 + rank * (i + 2)] for i in range(2)]
    zero16 = jnp.zeros((rank, rows), F32)
    hp = lt[0:64] + SCALE * dot(gm, jnp.concatenate([xa, zero16, zero16, zero16], 0), precision=HI)
    hb = hp[0:rank]
    hg = hp[48:56] + hp[56:64]
    gm8 = gm[48:56] + gm[56:64]
    stacks = [
        jnp.concatenate([xv[0], xa, zero16, zero16], 0),
        jnp.concatenate([xv[1], zero16, xa, zero16], 0),
    ]
    dhg = [SCALE * dot(gm8, st, precision=HI) for st in stacks]
    mk = [
        SCALE / model * jnp.sum(xv[i] * hb + xa * hp[rank * (i + 1):rank * (i + 2)], 0, keepdims=True)
        for i in range(2)
    ]
    pick = (
        lax.broadcasted_iota(jnp.int32, (8, 4), 0) == lax.broadcasted_iota(jnp.int32, (8, 4), 1)
    ).astype(F32)
    prior = dot(pick, prior_ref[...], NT, precision=HI)

    xa_cols = [part for part in split3(low)]
    shift = (
        lax.broadcasted_iota(jnp.int32, (lanes, rank), 0) == lax.broadcasted_iota(jnp.int32, (lanes, rank), 1) + 64
    ).astype(F32).astype(BF16)
    spread = dot(shift, b_ref[...]).astype(BF16)
    ssend[...] = jnp.zeros_like(ssend)
    for c in range(chunks):
        for f in range(2):
            for direction in range(2):
                wait_n(f, c, direction, 1)
                wait_n(f, c, direction, 2)
            at = slice(f * half + c * tc, f * half + (c + 1) * tc)
            ad = dot(xa_cols[0][at], spread) + dot(xa_cols[1][at], spread) + dot(xa_cols[2][at], spread)
            parts = []
            for part in range(2):
                parts.append(
                    tb[f, pos[f][0] * N + pos[f][1], part, c * tc:(c + 1) * tc, :].astype(F32)
                    + r2[f, c, part, 2].astype(F32)
                    + r2[f, c, 1 - part, 1].astype(F32)
                )
            h = jnp.concatenate(parts, 1) + rbuf[at, :].astype(F32) + SCALE * ad
            hi = h.astype(BF16)
            hhi[at, :] = hi
            hlo[at, :] = (h - hi.astype(F32)).astype(BF16)
            sq = h * h
            sq = sq[:, :lanes] + sq[:, lanes:]
            n = f * chunks + c
            ssend[n:n + 1, :] = jnp.sum(sq.T, 0, keepdims=True)

    ins = [send(ssend, sx.at[o - 1], c3s.at[o - 1], c3r.at[o - 1], xpeer[o]) for o in range(1, N)]
    for copy in ins:
        copy.wait_recv()
    sc[0] = ssend[...] + sx[0] + sx[1] + sx[2]
    ins = [send(sc.at[0], sy.at[o - 1], c3s.at[2 + o], c3r.at[2 + o], ypeer[o]) for o in range(1, N)]
    for copy in ins:
        copy.wait_recv()
    sc[1] = sc[0] + sy[0] + sy[1] + sy[2]
    send(sc.at[1], sc.at[2], c3s.at[6], c3r.at[6], sibling).wait_recv()
    stot = sc[1] + sc[2]
    square = jnp.concatenate([stot[i:i + 1, :] for i in range(2 * chunks)], 1)

    r = lax.rsqrt(square / model + EPS)
    r3 = r * r * r
    live = lax.broadcasted_iota(jnp.int32, (8, rows), 0) < 4
    logits = jnp.where(live, r * hg + prior, -1e30)
    ex = jnp.where(live, jnp.exp(logits - jnp.max(logits, 0, keepdims=True)), 0.0)
    p = ex / jnp.sum(ex, 0, keepdims=True)
    us, cs, t1 = [], [], []
    gcol = gm[0:rank]
    for i in range(2):
        dl = r * dhg[i] - r3 * mk[i] * hg
        q = p * (dl - jnp.sum(p * dl, 0, keepdims=True)) / total_tokens
        s = jnp.sum(q * hg, 0, keepdims=True) / model
        back = dot(gcol, jnp.concatenate([zero16, zero16, zero16, q, q], 0), precision=HI)
        us.append(SCALE * (r * back - r3 * s * hb))
        cs.append(r3 * s * xa)
        t1.append(dot(xa, r * q, NT, precision=HI))
    uu = jnp.concatenate(split3(jnp.concatenate(us, 0)), 0)
    cc = jnp.concatenate(split3(jnp.concatenate(cs, 0)), 0)
    n32 = 2 * rank

    def fold(m):
        return m[0:n32] + m[n32:2 * n32] + m[2 * n32:3 * n32]

    ggn = fold(dot(uu, xbuf[0]))
    ch = fold(dot(cc, hhi[...]) + dot(cc, hlo[...]))
    curv = SCALE * (dot(jnp.concatenate(t1, 0), g8[...], precision=HI) - ch)

    zw = 3 * lanes
    for i in range(4):
        at = slice(8 * i, 8 * i + 8)
        zpart[2 * i] = ggn[at, 0:zw]
        zpart[2 * i + 1, :, 0:piece - zw] = ggn[at, zw:piece]
        zpart[2 * i + 1, :, lanes:zw] = curv[at, :]
    ins = []
    for o in range(1, zs):
        ins.append(send(zpart.at[lax.rem(zi + o, zs)], zrecv.at[o - 1], zss.at[0, o - 1], zsr.at[0, o - 1], zpeer[o]))
    for copy in ins:
        copy.wait_recv()
    total = zpart[zi]
    for o in range(1, zs):
        total = total + zrecv[o - 1]
    zfull[zi] = total
    ins = [
        send(zfull.at[zi], zfull.at[zi], zss.at[1, o - 1], zsr.at[1, o - 1], zpeer[o]) for o in range(1, zs)
    ]
    for copy in ins:
        copy.wait_recv()
    for i in range(4):
        at = slice(8 * i, 8 * i + 8)
        ggn_ref[at, 0:zw] = zfull[2 * i]
        ggn_ref[at, zw:piece] = zfull[2 * i + 1, :, 0:piece - zw]
        curv_ref[at, :] = zfull[2 * i + 1, :, lanes:zw]
    for copy in sends:
        copy.wait_send()


def shards(zs, x, res, w, a_in, b_out, gain, head, prior, v_in, d_out):
    rows, piece = x.shape
    fb = res.shape[1]
    rank = a_in.shape[0]
    k = v_in.shape[0]
    chunks = 3
    half = rows // 2
    tc = half // chunks
    vmem = pl.BlockSpec(memory_space=pltpu.VMEM)
    hbm = pl.BlockSpec(memory_space=pl.ANY)
    dma = pltpu.SemaphoreType.DMA
    ggn, curv = pl.pallas_call(
        functools.partial(kernel, chunks, zs, rows * zs),
        out_shape=(
            jax.ShapeDtypeStruct((k * rank, piece), F32),
            jax.ShapeDtypeStruct((k * rank, fb), F32),
        ),
        in_specs=[hbm, hbm, hbm] + [vmem] * 7,
        out_specs=(vmem, vmem),
        scratch_shapes=[
            pltpu.VMEM((2, rows, piece), BF16),
            pltpu.VMEM((rows, fb), BF16),
            pltpu.VMEM((2, N * N, piece, fb), BF16),
            pltpu.VMEM((2, N * N, 2, half, 128), BF16),
            pltpu.VMEM((2, chunks, 2, 3, 2, 2, tc, 128), BF16),
            pltpu.VMEM((2, chunks, 2, 3, tc, 128), BF16),
            pltpu.VMEM((N, N, 128, fb), BF16),
            pltpu.VMEM((8, fb), F32),
            pltpu.VMEM((128, piece), BF16),
            pltpu.VMEM((2, piece, 128), F32),
            pltpu.VMEM((2, 64, 128), F32),
            pltpu.VMEM((rows, 128), F32),
            pltpu.VMEM((half, 128), F32),
            pltpu.VMEM((half, 128), F32),
            pltpu.VMEM((N - 1, half // N, 128), F32),
            pltpu.VMEM((N - 1, half // N // N, 128), F32),
            pltpu.VMEM((2, N, N, half // N // N, 128), F32),
            pltpu.VMEM((rows, fb), BF16),
            pltpu.VMEM((rows, fb), BF16),
            pltpu.VMEM((8, 128), F32),
            pltpu.VMEM((N - 1, 8, 128), F32),
            pltpu.VMEM((N - 1, 8, 128), F32),
            pltpu.VMEM((3, 8, 128), F32),
            pltpu.VMEM((8, 8, 384), F32),
            pltpu.VMEM((zs - 1, 8, 384), F32),
            pltpu.VMEM((8, 8, 384), F32),
            dma((N * N,)), dma((2,)), dma((1,)),
            dma((N * N,)), dma((N * N,)), dma((2,)), dma((2,)),
            dma((2, chunks, 2, 3)), dma((2, chunks, 2, 3)),
            dma((2, chunks, 2, 3)), dma((2, chunks, 2, 3)),
            dma((2, N - 1)), dma((2, N - 1)),
            dma((15,)), dma((15,)), dma((7,)), dma((7,)),
            dma((2, zs - 1)), dma((2, zs - 1)),
        ],
        compiler_params=pltpu.CompilerParams(
            collective_id=0, has_side_effects=True, vmem_limit_bytes=56 * 1024 * 1024
        ),
    )(
        x, res, w, a_in, b_out, gain.reshape(1, fb), head, prior,
        v_in.reshape(k * rank, piece), d_out.reshape(k * rank, fb),
    )
    return ggn.reshape(k, rank, piece), curv.reshape(k, rank, fb)


def solution(mesh):
    placed = (
        P("item", "tensor"),
        P("item", "tensor"),
        P("tensor", None),
        P(None, "tensor"),
        P(None, "tensor"),
        P("tensor"),
        P(None, "tensor"),
        P("item", None),
        P(None, None, "tensor"),
        P(None, None, "tensor"),
    )
    return jax.shard_map(
        functools.partial(shards, mesh.shape["item"]),
        mesh=mesh,
        in_specs=placed,
        out_specs=(P(None, None, "tensor"), P(None, None, "tensor")),
        check_vma=False,
    )
```

time: 422 us -> 97.4 us (0.23)
  waiting for transfers between devices: 288 us -> 0 us
  Pallas kernels: 0 us -> 87.4 us
  blocking collectives: 79.7 us -> 0 us
  matrix products: 30.6 us -> 0 us
  between operations: 14 us -> 0.64 us
  other arithmetic: 5.61 us -> 0 us
  local copies, waits for them, and re-layouts: 3.11 us -> 7.96 us
    psum x2 -> x0, waiting for transfers between devices: 177 us -> none  [the longest x1 98.7 us: shards(): low = lax.psum(jnp.concatenate([low, hp], 1), 'tensor')]
    reduce_scatter x1 -> x0, waiting for transfers between devices: 111 us -> none  [shards(): lax.psum_scatter(term, 'tensor', scatter_dimension=1, tiled=True)]
    pallas_call x0 -> x1, Pallas kernels: none -> 87.4 us  [shards(): pl.pallas_call(functools.partial(kernel, chunks, zs, rows * zs), out_shap...]
    psum x1 -> x0, blocking collectives: 54.1 us -> none  [shards(): sq = lax.psum(jnp.sum(h * h, 1), 'tensor')]
    dot_general x22 -> x0, matrix products: 30.6 us -> none  [the longest x1 12.7 us: shards(): term = jnp.dot(x, w, preferred_element_type=f32).astype(jnp.bfloat16)]
    all_gather x1 -> x0, blocking collectives: 25.6 us -> none  [shards(): full = lax.all_gather(proj, 'tensor', axis=1, tiled=True)]
    unnamed x14 -> x4, local copies, waits for them, and re-layouts: 0.03 us -> 6.74 us
  transfers between devices with their start and end apart: 3 -> 0, of which waited for: 3 -> 0; matrix products, arithmetic and copies ran while one was open for 4% -> 0% of each run, Pallas kernels for 0% -> 0%
where the time goes in v2:
time: 97.4 us; the launch traced here: 96 us
  Pallas kernels  87.4 us (90%)
  local copies, waits for them, and re-layouts  7.96 us (8%)
    pallas_call x1, Pallas kernels, shards(): pl.pallas_call(functools.partial(kernel, chunks, zs, rows * zs), out_shap...  87.4 us
    unnamed x4, local copies, waits for them, and re-layouts  6.74 us

profile of v2, /device:TPU:2, one launch (start us, length us, event | category | flops | bytes accessed | tf_op | source)
XLA Modules:
  0.0 96.0 jit_solution(14454560647703858408)
XLA Ops:
  0.6 1.2 %reshape.19.g_ref = bf16[1,256]{1,0:T(2,128)(2,1)} reshape(bf16[256]{0:T(256)(128)(2,1)} %param.15) | data formatting | bytes 1024 | tf_op jit(solution)/shard_map/reshape | solution.py:515
  1.9 1.6 %copy.13.prior_ref = f32[768,4]{1,0:T(8,128)} copy(f32[768,4]{0,1:T(4,128)} %param.17) | data formatting | bytes 24576 | tf_op args[7]
  3.5 2.3 %copy.12.x_hbm = bf16[768,448]{1,0:T(8,128)(2,1)} copy(bf16[768,448]{0,1:T(8,128)(2,1)} %param.10) | data formatting | bytes 1376256 | tf_op args[0]
  5.7 87.4 %shard_map.113 = (f32[32,448]{1,0:T(8,128)}, f32[32,256]{1,0:T(8,128)}) custom-call(bf16[768,448]{1,0:T(8,128)(2,1)} %copy.12.x_hbm, bf16[768,256]{1,0:T(8,128)(2,1)} %r_hbm.1, bf16[448,8192]{1,0:T(8,128)(2,1)} %w_hbm.1, bf16[16,448]{1,0:T(8,128)(2,1)} %a_ref.1, bf16[16,256]{1,0:T(8,128)(2,1)} %b_ref.1, bf16[1,256]{1,0:T(2,128)(2,1)} %reshape.19.g_ref, ...), custom_call_target="tpu_custom_call" | custom-call | tf_op jit(solution)/shard_map/pallas_call | solution.py:468
  93.2 1.5 %copy.16 = f32[2,16,448]{2,1,0:T(8,128)} copy(f32[2,16,448]{2,1,0:T(8,128)} %bitcast.4) | data formatting | bytes 114688
  94.6 1.4 %copy.17 = f32[2,16,256]{2,1,0:T(8,128)} copy(f32[2,16,256]{2,1,0:T(8,128)} %bitcast.6) | data formatting | bytes 65536

commit v3 on v2

--- a/solution.py
+++ b/solution.py
@@ -36,12 +36,12 @@
 def kernel(
     chunks, zs, total_tokens,
     x_hbm, r_hbm, w_hbm, a_ref, b_ref, g_ref, head_ref, prior_ref, v_ref, d_ref,
-    ggn_ref, curv_ref,
-    xbuf, rbuf, wbuf, tb, r1, r2, pf, g8, avp, ybuf, gram, lbuf, la, lc, lx, ly, lfull,
-    hhi, hlo, ssend, sx, sy, sc, zpart, zrecv, zfull,
+    out_ref,
+    xt, xbuf, rbuf, wbuf, tb, r1, r2, pf, g8, avp, ybuf, gram, lbuf, la, lc, lx, lfull,
+    hhi, hlo, ssend, sx, zpart, zrecv, zfull,
     wl, xl, rl, ws, wr, xs, xr, ms, mr, ns, nr, c1s, c1r, c2s, c2r, c3s, c3r, zss, zsr,
 ):
-    rows, piece = x_hbm.shape
+    piece, rows = x_hbm.shape
     half = rows // 2
     tc = half // chunks
     fb = r_hbm.shape[1]
@@ -62,6 +62,18 @@
     xpeer = [None] + [device(wrap(px + o), py, core) for o in range(1, N)]
     ypeer = [None] + [device(px, wrap(py + o), core) for o in range(1, N)]
     zpeer = [None] + [{"item": lax.rem(zi + o, zs)} for o in range(1, zs)]
+
+    def far(i, j, c=0):
+        return min(i, N - i) + min(j, N - j) + 0.1 * c
+
+    plane = [(i, j, c) for i in range(N) for j in range(N) for c in range(2)][1:]
+    plane.sort(key=lambda o: -far(*o))
+    same = [o for o in plane if o[2] == 0]
+    zorder = sorted(range(1, zs), key=lambda o: -min(o, zs - o))
+
+    def away(o):
+        return device(wrap(px + o[0]), wrap(py + o[1]), lax.rem(core + o[2], 2))
+
     sends = []
 
     def send(src, dst, ssem, rsem, to):
@@ -83,7 +95,7 @@
         return pl.ds(pl.multiple_of((b * 2 + c) * fb, fb), fb)
 
     xloads = [
-        pltpu.make_async_copy(x_hbm.at[pl.ds(f * half, half)], xbuf.at[0, pl.ds(f * half, half)], xl.at[f])
+        pltpu.make_async_copy(x_hbm.at[:, pl.ds(f * half, half)], xt.at[0, :, pl.ds(f * half, half)], xl.at[f])
         for f in range(2)
     ]
     wloads = [
@@ -100,7 +112,7 @@
     rload.start()
 
     g8[...] = jnp.zeros_like(g8)
-    g8[0:4, :] = head_ref[...].astype(F32) * g_ref[...].astype(F32)
+    g8[0:4, :] = head_ref[...].astype(F32) * g_ref[...].astype(F32).reshape(1, fb)
     ghi = g8[...].astype(BF16).astype(F32)
     pf[:, :, 64:128, :] = jnp.zeros((N, N, 64, fb), BF16)
     pf[py, px, 0:rank, :] = b_ref[...]
@@ -111,13 +123,13 @@
     avp[64 + rank:64 + 3 * rank, :] = v_ref[...]
 
     barrier = pltpu.get_barrier_semaphore()
-    peers = [sibling] + xpeer[1:] + ypeer[1:] + zpeer[1:]
+    peers = [away(o) for o in plane] + zpeer[1:]
     for to in peers:
         pl.semaphore_signal(barrier, inc=1, device_id=to, device_id_type=pl.DeviceIdType.MESH)
     pl.semaphore_wait(barrier, len(peers))
 
     def send_x(f):
-        return send(x_hbm.at[pl.ds(f * half, half)], xbuf.at[1, pl.ds(f * half, half)], xs.at[f], xr.at[f], sibling)
+        return send(x_hbm.at[:, pl.ds(f * half, half)], xt.at[1, :, pl.ds(f * half, half)], xs.at[f], xr.at[f], sibling)
 
     def send_w(n):
         return send(w_hbm.at[:, columns(block(n), 1 - core)], wbuf.at[1, block(n)], ws.at[n], wr.at[n], sibling)
@@ -136,7 +148,16 @@
 
     pos = [(px, py), (py, px)]
 
-    def group(f, i1):
+    eye = (
+        lax.broadcasted_iota(jnp.int32, (lanes, lanes), 0) == lax.broadcasted_iota(jnp.int32, (lanes, lanes), 1)
+    ).astype(F32).astype(BF16)
+
+    def turn(s, f):
+        for i in range(half // lanes):
+            at = slice(f * half + i * lanes, f * half + (i + 1) * lanes)
+            xbuf[s, at, :] = dot(eye, xt[s, :, at], NT).astype(BF16)
+
+    def group(f, i1, lo=0, hi=N):
         def body(i2, carry):
             b = i1 * N + i2 if f == 0 else i2 * N + i1
             acc = dot(xbuf[0, f * half:(f + 1) * half, :], wbuf[0, b])
@@ -146,12 +167,7 @@
             tb[f, i1 * N + i2, 1] = out[:, lanes:]
             return carry
 
-        lax.fori_loop(0, N, body, 0)
-
-    def step1(f, o):
-        p1 = wrap(pos[f][0] + o)
-        peer = xpeer if f == 0 else ypeer
-        return p1, peer
+        lax.fori_loop(lo, hi, body, 0)
 
     def send_m(f, c, direction, msg):
         peer = xpeer if f == 0 else ypeer
@@ -187,36 +203,43 @@
         wloads[n].wait()
         win[n].wait_recv()
 
-    xloads[0].wait()
-    xin[0].wait_recv()
+    def first(f):
+        xloads[f].wait()
+        turn(0, f)
+        xin[f].wait_recv()
+        turn(1, f)
+
+    def start(f):
+        for direction in range(2):
+            group(f, wrap(pos[f][0] + 2), 2 * direction, 2 * direction + 2)
+            for c in range(chunks):
+                send_m(f, c, direction, 0)
+
+    first(0)
     for n in range(N):
         wait_w(n)
-    group(0, wrap(px + 2))
-    for c in range(chunks):
-        for direction in range(2):
-            send_m(0, c, direction, 0)
+    start(0)
     for copy in pin:
         copy.wait_recv()
     pin2 = [
         send(pf.at[py, :, pl.ds(0, 64)], pf.at[py, :, pl.ds(0, 64)], c1s.at[1, o - 1], c1r.at[1, o - 1], ypeer[o])
         for o in range(1, N)
     ]
-    xloads[1].wait()
-    xin[1].wait_recv()
+    first(1)
     for n in range(N, 2 * N - 1):
         wait_w(n)
-    group(1, wrap(py + 2))
-    for c in range(chunks):
-        for direction in range(2):
-            send_m(1, c, direction, 0)
+    start(1)
     for n in range(2 * N - 1, N * N):
         wait_w(n)
+
+    def send_m2(f, c):
+        for direction in range(2):
+            send_m(f, c, direction, 1)
+
     for f in range(2):
         group(f, wrap(pos[f][0] + 1))
         group(f, wrap(pos[f][0] + N - 1))
-        for c in range(chunks):
-            for direction in range(2):
-                send_m(f, c, direction, 1)
+        send_m2(f, 0)
 
     def middle(f, c):
         for direction in range(2):
@@ -227,17 +250,19 @@
             send_m(f, c, direction, 2)
 
     for f in range(2):
-        group(f, pos[f][0])
-    for c in range(chunks):
-        for f in range(2):
-            middle(f, c)
+        middle(f, 0)
+        send_m2(f, 1)
+    group(0, pos[0][0])
+    for f in range(2):
+        middle(f, 1)
+        send_m2(f, 2)
+    group(1, pos[1][0])
 
     for copy in pin2:
         copy.wait_recv()
-    eye = (
-        lax.broadcasted_iota(jnp.int32, (piece, piece), 0) == lax.broadcasted_iota(jnp.int32, (piece, piece), 1)
-    ).astype(F32).astype(BF16)
-    ybuf[0] = dot(eye, avp[...], NT)
+    for i in range(piece // 64):
+        at = slice(i * 64, (i + 1) * 64)
+        ybuf[0, at, :] = dot(eye[0:64, 0:64], avp[:, at], NT)
     ybuf[1] = jnp.zeros((piece, lanes), F32)
     gram[0] = jnp.zeros((64, lanes), F32)
 
@@ -249,7 +274,10 @@
         gram[0] = gram[0] + dot(p[0:64], p, NT)
         return carry
 
-    lax.fori_loop(0, N * N, project, 0)
+    lax.fori_loop(0, N * N // 2, project, 0)
+    for f in range(2):
+        middle(f, 2)
+    lax.fori_loop(N * N // 2, N * N, project, 0)
     rload.wait()
     for s in range(2):
         for i, part in enumerate(split3(ybuf[s])):
@@ -290,44 +318,35 @@
             tb[at] = (tb[at].astype(F32) + r2[f, c, direction, 0].astype(F32)).astype(BF16)
             send_n(f, c, direction, 2)
 
+    for f in range(2):
+        stage2(f, 0)
     lin.wait_recv()
     lc[...] = lbuf[pl.ds(mine, half), :] + la[...]
-    q1, q2 = half // N, half // N // N
-
-    def xslice(o):
-        return pl.ds(pl.multiple_of(wrap(px + o) * q1, q1), q1)
-
-    bins = [send(lc.at[xslice(o)], lx.at[o - 1], c2s.at[1 + o], c2r.at[1 + o], xpeer[o]) for o in range(1, N)]
-    for f in range(2):
-        stage2(f, 0)
-    for copy in bins:
-        copy.wait_recv()
-    lc[xslice(0), :] = lc[xslice(0), :] + lx[0] + lx[1] + lx[2]
-
-    def yslice(o):
-        return pl.ds(pl.multiple_of(px * q1 + wrap(py + o) * q2, q2), q2)
-
-    cins = [send(lc.at[yslice(o)], ly.at[o - 1], c2s.at[4 + o], c2r.at[4 + o], ypeer[o]) for o in range(1, N)]
+    q = half // (N * N)
+
+    def part_of(o):
+        return pl.ds(pl.multiple_of((wrap(px + o[0]) * N + wrap(py + o[1])) * q, q), q)
+
+    bins = [send(lc.at[part_of(o)], lx.at[i], c2s.at[2 + i], c2r.at[2 + i], away(o)) for i, o in enumerate(same)]
+    for f in range(2):
+        stage2(f, 1)
     for f in range(2):
         stage3(f, 0)
-        stage2(f, 1)
-    for copy in cins:
-        copy.wait_recv()
-    lfull[core, px, py] = lc[yslice(0), :] + ly[0] + ly[1] + ly[2]
+    total = lc[part_of((0, 0)), :]
+    for i, copy in enumerate(bins):
+        copy.wait_recv()
+        total = total + lx[i]
+    lfull[core, px, py] = total
     own = lfull.at[core, px, py]
-    dins = [send(own, own, c2s.at[7 + o], c2r.at[7 + o], ypeer[o]) for o in range(1, N)]
+    dins = [send(own, own, c2s.at[17 + i], c2r.at[17 + i], away(o)) for i, o in enumerate(same)]
+    for f in range(2):
+        stage2(f, 2)
     for f in range(2):
         stage3(f, 1)
     for copy in dins:
         copy.wait_recv()
-    own = lfull.at[core, px]
-    eins = [send(own, own, c2s.at[10 + o], c2r.at[10 + o], xpeer[o]) for o in range(1, N)]
-    for f in range(2):
-        stage2(f, 2)
-    for copy in eins:
-        copy.wait_recv()
     own = lfull.at[core]
-    fin = send(own, own, c2s.at[14], c2r.at[14], sibling)
+    fin = send(own, own, c2s.at[32], c2r.at[32], sibling)
     for f in range(2):
         stage3(f, 2)
     fin.wait_recv()
@@ -352,10 +371,7 @@
         SCALE / model * jnp.sum(xv[i] * hb + xa * hp[rank * (i + 1):rank * (i + 2)], 0, keepdims=True)
         for i in range(2)
     ]
-    pick = (
-        lax.broadcasted_iota(jnp.int32, (8, 4), 0) == lax.broadcasted_iota(jnp.int32, (8, 4), 1)
-    ).astype(F32)
-    prior = dot(pick, prior_ref[...], NT, precision=HI)
+    prior = jnp.concatenate([prior_ref[...], jnp.zeros((4, rows), F32)], 0)
 
     xa_cols = [part for part in split3(low)]
     shift = (
@@ -386,16 +402,11 @@
             n = f * chunks + c
             ssend[n:n + 1, :] = jnp.sum(sq.T, 0, keepdims=True)
 
-    ins = [send(ssend, sx.at[o - 1], c3s.at[o - 1], c3r.at[o - 1], xpeer[o]) for o in range(1, N)]
-    for copy in ins:
-        copy.wait_recv()
-    sc[0] = ssend[...] + sx[0] + sx[1] + sx[2]
-    ins = [send(sc.at[0], sy.at[o - 1], c3s.at[2 + o], c3r.at[2 + o], ypeer[o]) for o in range(1, N)]
-    for copy in ins:
-        copy.wait_recv()
-    sc[1] = sc[0] + sy[0] + sy[1] + sy[2]
-    send(sc.at[1], sc.at[2], c3s.at[6], c3r.at[6], sibling).wait_recv()
-    stot = sc[1] + sc[2]
+    ins = [send(ssend, sx.at[i], c3s.at[i], c3r.at[i], away(o)) for i, o in enumerate(plane)]
+    stot = ssend[...]
+    for i, copy in enumerate(ins):
+        copy.wait_recv()
+        stot = stot + sx[i]
     square = jnp.concatenate([stot[i:i + 1, :] for i in range(2 * chunks)], 1)
 
     r = lax.rsqrt(square / model + EPS)
@@ -432,7 +443,7 @@
         zpart[2 * i + 1, :, 0:piece - zw] = ggn[at, zw:piece]
         zpart[2 * i + 1, :, lanes:zw] = curv[at, :]
     ins = []
-    for o in range(1, zs):
+    for o in zorder:
         ins.append(send(zpart.at[lax.rem(zi + o, zs)], zrecv.at[o - 1], zss.at[0, o - 1], zsr.at[0, o - 1], zpeer[o]))
     for copy in ins:
         copy.wait_recv()
@@ -441,17 +452,23 @@
         total = total + zrecv[o - 1]
     zfull[zi] = total
     ins = [
-        send(zfull.at[zi], zfull.at[zi], zss.at[1, o - 1], zsr.at[1, o - 1], zpeer[o]) for o in range(1, zs)
+        send(zfull.at[zi], zfull.at[zi], zss.at[1, o - 1], zsr.at[1, o - 1], zpeer[o]) for o in zorder
     ]
     for copy in ins:
         copy.wait_recv()
+    out_ref[...] = zfull[...]
+    for copy in sends:
+        copy.wait_send()
+
+
+def unpack(in_ref, ggn_ref, curv_ref):
+    zw = in_ref.shape[2]
+    piece = ggn_ref.shape[1]
     for i in range(4):
         at = slice(8 * i, 8 * i + 8)
-        ggn_ref[at, 0:zw] = zfull[2 * i]
-        ggn_ref[at, zw:piece] = zfull[2 * i + 1, :, 0:piece - zw]
-        curv_ref[at, :] = zfull[2 * i + 1, :, lanes:zw]
-    for copy in sends:
-        copy.wait_send()
+        ggn_ref[at, 0:zw] = in_ref[2 * i]
+        ggn_ref[at, zw:piece] = in_ref[2 * i + 1, :, 0:piece - zw]
+        curv_ref[at, :] = in_ref[2 * i + 1, :, 128:zw]
 
 
 def shards(zs, x, res, w, a_in, b_out, gain, head, prior, v_in, d_out):
@@ -462,18 +479,17 @@
     chunks = 3
     half = rows // 2
     tc = half // chunks
+    q = half // N // N
     vmem = pl.BlockSpec(memory_space=pltpu.VMEM)
     hbm = pl.BlockSpec(memory_space=pl.ANY)
     dma = pltpu.SemaphoreType.DMA
-    ggn, curv = pl.pallas_call(
+    packed = pl.pallas_call(
         functools.partial(kernel, chunks, zs, rows * zs),
-        out_shape=(
-            jax.ShapeDtypeStruct((k * rank, piece), F32),
-            jax.ShapeDtypeStruct((k * rank, fb), F32),
-        ),
+        out_shape=jax.ShapeDtypeStruct((8, 8, 384), F32),
         in_specs=[hbm, hbm, hbm] + [vmem] * 7,
-        out_specs=(vmem, vmem),
+        out_specs=vmem,
         scratch_shapes=[
+            pltpu.VMEM((2, piece, rows), BF16),
             pltpu.VMEM((2, rows, piece), BF16),
             pltpu.VMEM((rows, fb), BF16),
             pltpu.VMEM((2, N * N, piece, fb), BF16),
@@ -488,15 +504,12 @@
             pltpu.VMEM((rows, 128), F32),
             pltpu.VMEM((half, 128), F32),
             pltpu.VMEM((half, 128), F32),
-            pltpu.VMEM((N - 1, half // N, 128), F32),
-            pltpu.VMEM((N - 1, half // N // N, 128), F32),
-            pltpu.VMEM((2, N, N, half // N // N, 128), F32),
+            pltpu.VMEM((N * N - 1, q, 128), F32),
+            pltpu.VMEM((2, N, N, q, 128), F32),
             pltpu.VMEM((rows, fb), BF16),
             pltpu.VMEM((rows, fb), BF16),
             pltpu.VMEM((8, 128), F32),
-            pltpu.VMEM((N - 1, 8, 128), F32),
-            pltpu.VMEM((N - 1, 8, 128), F32),
-            pltpu.VMEM((3, 8, 128), F32),
+            pltpu.VMEM((2 * N * N - 1, 8, 128), F32),
             pltpu.VMEM((8, 8, 384), F32),
             pltpu.VMEM((zs - 1, 8, 384), F32),
             pltpu.VMEM((8, 8, 384), F32),
@@ -505,16 +518,23 @@
             dma((2, chunks, 2, 3)), dma((2, chunks, 2, 3)),
             dma((2, chunks, 2, 3)), dma((2, chunks, 2, 3)),
             dma((2, N - 1)), dma((2, N - 1)),
-            dma((15,)), dma((15,)), dma((7,)), dma((7,)),
+            dma((33,)), dma((33,)), dma((2 * N * N - 1,)), dma((2 * N * N - 1,)),
             dma((2, zs - 1)), dma((2, zs - 1)),
         ],
         compiler_params=pltpu.CompilerParams(
             collective_id=0, has_side_effects=True, vmem_limit_bytes=56 * 1024 * 1024
         ),
     )(
-        x, res, w, a_in, b_out, gain.reshape(1, fb), head, prior,
+        x.T, res, w, a_in, b_out, gain, head, prior.T,
         v_in.reshape(k * rank, piece), d_out.reshape(k * rank, fb),
     )
+    ggn, curv = pl.pallas_call(
+        unpack,
+        out_shape=(
+            jax.ShapeDtypeStruct((k * rank, piece), F32),
+            jax.ShapeDtypeStruct((k * rank, fb), F32),
+        ),
+    )(packed)
     return ggn.reshape(k, rank, piece), curv.reshape(k, rank, fb)
 
 

time: 97.4 us -> 82.9 us (0.85); the launches traced: 96 us -> 82.7 us
  local copies, waits for them, and re-layouts: 7.96 us -> 0 us
  Pallas kernels: 87.4 us -> 82 us
    pallas_call x1, Pallas kernels: 87.4 us -> 80.5 us  [shards(): pl.pallas_call(functools.partial(kernel, chunks, zs, rows * zs), out_shap...]
    unnamed x4 -> x0, local copies, waits for them, and re-layouts: 6.74 us -> none
    pallas_call x0 -> x1, Pallas kernels: none -> 1.54 us  [shards(): pl.pallas_call(unpack, out_shape=(jax.ShapeDtypeStruct((k * rank, piece),...]
    reshape x1 -> x0, local copies, waits for them, and re-layouts: 1.22 us -> none  [shards(): gain.reshape(1, fb)]
where the time goes in v3:
time: 82.9 us; the launch traced here: 82.7 us
  Pallas kernels  82 us (99%)
    pallas_call x1, Pallas kernels, shards(): pl.pallas_call(functools.partial(kernel, chunks, zs, rows * zs), out_shap...  80.5 us

profile of v3, /device:TPU:2, one launch (start us, length us, event | category | flops | bytes accessed | tf_op | source)
XLA Modules:
  0.0 82.7 jit_solution(5904951690060551197)
XLA Ops:
  0.6 80.5 %shard_map.113.in_ref = f32[8,8,384]{2,1,0:T(8,128)} custom-call(bf16[448,768]{1,0:T(8,128)(2,1)} %bitcast.6, bf16[768,256]{1,0:T(8,128)(2,1)} %r_hbm.1, bf16[448,8192]{1,0:T(8,128)(2,1)} %w_hbm.1, bf16[16,448]{1,0:T(8,128)(2,1)} %a_ref.1, bf16[16,256]{1,0:T(8,128)(2,1)} %b_ref.1, bf16[256]{0:T(256)(128)(2,1)} %g_ref.1, bf16[4,256]{1,0:T(4,128)(2,1)} %head_ref.1, ...), custom_call_target="tpu_custom_call" | custom-call | tf_op jit(solution)/shard_map/pallas_call | solution.py:486
  81.1 1.5 %shard_map.114 = (f32[32,448]{1,0:T(8,128)}, f32[32,256]{1,0:T(8,128)}) custom-call(f32[8,8,384]{2,1,0:T(8,128)} %shard_map.113.in_ref), custom_call_target="tpu_custom_call" | custom-call | tf_op jit(solution)/shard_map/pallas_call | solution.py:531

commit v4 on v3

--- a/solution.py
+++ b/solution.py
@@ -35,9 +35,10 @@
 
 def kernel(
     chunks, zs, total_tokens,
-    x_hbm, r_hbm, w_hbm, a_ref, b_ref, g_ref, head_ref, prior_ref, v_ref, d_ref,
+    x_hbm, r_hbm, w_hbm, a_hbm, b_hbm, g_hbm, head_hbm, prior_hbm, v_hbm, d_hbm,
     out_ref,
-    xt, xbuf, rbuf, wbuf, tb, r1, r2, pf, g8, avp, ybuf, gram, lbuf, la, lc, lx, lfull,
+    a_ref, b_ref, g_ref, head_ref, prior_ref, v_ref, d_ref, sl,
+    xt, xbuf, rbuf, wbuf, tb, r1, r2, pf, pown, g8, avp, ybuf, yin, gram, lbuf, la, lc, lx, lfull,
     hhi, hlo, ssend, sx, zpart, zrecv, zfull,
     wl, xl, rl, ws, wr, xs, xr, ms, mr, ns, nr, c1s, c1r, c2s, c2r, c3s, c3r, zss, zsr,
 ):
@@ -47,7 +48,7 @@
     fb = r_hbm.shape[1]
     lanes = 128
     model = w_hbm.shape[1]
-    rank = a_ref.shape[0]
+    rank = a_hbm.shape[0]
     zi = lax.axis_index("item")
     me = lax.axis_index("tensor")
     core = lax.rem(me, 2)
@@ -85,6 +86,11 @@
         sends.append(copy)
         return copy
 
+    barrier = pltpu.get_barrier_semaphore()
+    peers = [away(o) for o in plane] + zpeer[1:]
+    for to in peers:
+        pl.semaphore_signal(barrier, inc=1, device_id=to, device_id_type=pl.DeviceIdType.MESH)
+
     order = [(2, o) for o in range(N)] + [(o, 2) for o in (0, 1, 3)]
     order += [(i, j) for i in (1, 3, 0) for j in (1, 3, 0)]
 
@@ -95,14 +101,23 @@
         return pl.ds(pl.multiple_of((b * 2 + c) * fb, fb), fb)
 
     xloads = [
-        pltpu.make_async_copy(x_hbm.at[:, pl.ds(f * half, half)], xt.at[0, :, pl.ds(f * half, half)], xl.at[f])
+        pltpu.make_async_copy(x_hbm.at[:, pl.ds(f * half, half)], xt.at[pl.ds(0, piece), pl.ds(f * half, half)], xl.at[f])
         for f in range(2)
     ]
     wloads = [
-        pltpu.make_async_copy(w_hbm.at[:, columns(block(n), core)], wbuf.at[0, block(n)], wl.at[n])
+        pltpu.make_async_copy(w_hbm.at[:, columns(block(n), core)], wbuf.at[block(n), pl.ds(0, piece)], wl.at[n])
         for n in range(N * N)
     ]
+    small = [
+        pltpu.make_async_copy(src, dst, sl.at[i])
+        for i, (src, dst) in enumerate([
+            (b_hbm, b_ref), (d_hbm, d_ref), (g_hbm, g_ref), (head_hbm, head_ref), (a_hbm, a_ref), (v_hbm, v_ref),
+            (prior_hbm, prior_ref),
+        ])
+    ]
     rload = pltpu.make_async_copy(r_hbm, rbuf, rl.at[0])
+    for copy in small:
+        copy.start()
     xloads[0].start()
     for n in range(N):
         wloads[n].start()
@@ -110,35 +125,34 @@
     for n in range(N, N * N):
         wloads[n].start()
     rload.start()
+    for copy in small:
+        copy.wait()
 
     g8[...] = jnp.zeros_like(g8)
     g8[0:4, :] = head_ref[...].astype(F32) * g_ref[...].astype(F32).reshape(1, fb)
     ghi = g8[...].astype(BF16).astype(F32)
     pf[:, :, 64:128, :] = jnp.zeros((N, N, 64, fb), BF16)
-    pf[py, px, 0:rank, :] = b_ref[...]
-    pf[py, px, rank:3 * rank, :] = d_ref[...]
-    pf[py, px, 3 * rank:64, :] = jnp.concatenate([ghi, g8[...] - ghi], 0).astype(BF16)
+    pown[64:128, :] = jnp.zeros((64, fb), BF16)
+    pown[0:rank, :] = b_ref[...]
+    pown[rank:3 * rank, :] = d_ref[...]
+    pown[3 * rank:64, :] = jnp.concatenate([ghi, g8[...] - ghi], 0).astype(BF16)
     avp[...] = jnp.zeros_like(avp)
     avp[64:64 + rank, :] = a_ref[...]
     avp[64 + rank:64 + 3 * rank, :] = v_ref[...]
 
-    barrier = pltpu.get_barrier_semaphore()
-    peers = [away(o) for o in plane] + zpeer[1:]
-    for to in peers:
-        pl.semaphore_signal(barrier, inc=1, device_id=to, device_id_type=pl.DeviceIdType.MESH)
+    pf[py, px, 0:64, :] = pown[0:64, :]
     pl.semaphore_wait(barrier, len(peers))
 
     def send_x(f):
-        return send(x_hbm.at[:, pl.ds(f * half, half)], xt.at[1, :, pl.ds(f * half, half)], xs.at[f], xr.at[f], sibling)
+        return send(x_hbm.at[:, pl.ds(f * half, half)], xt.at[pl.ds(piece, piece), pl.ds(f * half, half)], xs.at[f], xr.at[f], sibling)
 
     def send_w(n):
-        return send(w_hbm.at[:, columns(block(n), 1 - core)], wbuf.at[1, block(n)], ws.at[n], wr.at[n], sibling)
+        return send(w_hbm.at[:, columns(block(n), 1 - core)], wbuf.at[block(n), pl.ds(piece, piece)], ws.at[n], wr.at[n], sibling)
 
     xin = [send_x(0)]
     win = [send_w(n) for n in range(N)]
     pin = [
-        send(pf.at[py, px, pl.ds(0, 64)], pf.at[py, px, pl.ds(0, 64)], c1s.at[0, o - 1], c1r.at[0, o - 1], xpeer[o])
-        for o in range(1, N)
+        send(pown.at[pl.ds(0, 64)], pf.at[py, px, pl.ds(0, 64)], c1s.at[i], c1r.at[i], away(o)) for i, o in enumerate(same)
     ]
     xin.append(send_x(1))
     win += [send_w(n) for n in range(N, N * N)]
@@ -152,22 +166,41 @@
         lax.broadcasted_iota(jnp.int32, (lanes, lanes), 0) == lax.broadcasted_iota(jnp.int32, (lanes, lanes), 1)
     ).astype(F32).astype(BF16)
 
-    def turn(s, f):
+    def turn(f):
         for i in range(half // lanes):
             at = slice(f * half + i * lanes, f * half + (i + 1) * lanes)
-            xbuf[s, at, :] = dot(eye, xt[s, :, at], NT).astype(BF16)
+            xbuf[at, :] = dot(eye, xt[:, at], NT).astype(BF16)
+
+    def put(f, i1, i2, out):
+        tb[f, i1 * N + i2, 0] = out[:, :lanes]
+        tb[f, i1 * N + i2, 1] = out[:, lanes:]
 
     def group(f, i1, lo=0, hi=N):
         def body(i2, carry):
             b = i1 * N + i2 if f == 0 else i2 * N + i1
-            acc = dot(xbuf[0, f * half:(f + 1) * half, :], wbuf[0, b])
-            acc = acc + dot(xbuf[1, f * half:(f + 1) * half, :], wbuf[1, b])
-            out = acc.astype(BF16)
-            tb[f, i1 * N + i2, 0] = out[:, :lanes]
-            tb[f, i1 * N + i2, 1] = out[:, lanes:]
+            put(f, i1, i2, dot(xbuf[f * half:(f + 1) * half, :], wbuf[b]).astype(BF16))
             return carry
 
         lax.fori_loop(lo, hi, body, 0)
+
+    def both(count, ox, oy):
+        def body(n, carry):
+            x, y = wrap(px + ox(n)), wrap(py + oy(n))
+            out = dot(xbuf[...], wbuf[x * N + y]).astype(BF16)
+            put(0, x, y, out[:half])
+            put(1, y, x, out[half:])
+            return carry
+
+        lax.fori_loop(0, count, body, 0)
+
+    def single(f, offsets):
+        def body(n, carry):
+            i1, i2 = wrap(pos[f][0] + offsets(n)), wrap(pos[f][1] + 2)
+            b = i1 * N + i2 if f == 0 else i2 * N + i1
+            put(f, i1, i2, dot(xbuf[f * half:(f + 1) * half, :], wbuf[b]).astype(BF16))
+            return carry
+
+        return body
 
     def send_m(f, c, direction, msg):
         peer = xpeer if f == 0 else ypeer
@@ -205,9 +238,8 @@
 
     def first(f):
         xloads[f].wait()
-        turn(0, f)
         xin[f].wait_recv()
-        turn(1, f)
+        turn(f)
 
     def start(f):
         for direction in range(2):
@@ -219,12 +251,6 @@
     for n in range(N):
         wait_w(n)
     start(0)
-    for copy in pin:
-        copy.wait_recv()
-    pin2 = [
-        send(pf.at[py, :, pl.ds(0, 64)], pf.at[py, :, pl.ds(0, 64)], c1s.at[1, o - 1], c1r.at[1, o - 1], ypeer[o])
-        for o in range(1, N)
-    ]
     first(1)
     for n in range(N, 2 * N - 1):
         wait_w(n)
@@ -236,10 +262,13 @@
         for direction in range(2):
             send_m(f, c, direction, 1)
 
-    for f in range(2):
-        group(f, wrap(pos[f][0] + 1))
-        group(f, wrap(pos[f][0] + N - 1))
-        send_m2(f, 0)
+    both(4, lambda n: 1 + 2 * lax.div(n, 2), lambda n: 1 + 2 * lax.rem(n, 2))
+    both(2, lambda n: 1 + 2 * n, lambda n: 0)
+    lax.fori_loop(0, 2, single(0, lambda n: 1 + 2 * n), 0)
+    send_m2(0, 0)
+    both(2, lambda n: 0, lambda n: 1 + 2 * n)
+    lax.fori_loop(0, 2, single(1, lambda n: 1 + 2 * n), 0)
+    send_m2(1, 0)
 
     def middle(f, c):
         for direction in range(2):
@@ -252,47 +281,44 @@
     for f in range(2):
         middle(f, 0)
         send_m2(f, 1)
-    group(0, pos[0][0])
+    both(1, lambda n: n, lambda n: n)
+    for f in range(2):
+        lax.fori_loop(0, 1, single(f, lambda n: n), 0)
     for f in range(2):
         middle(f, 1)
         send_m2(f, 2)
-    group(1, pos[1][0])
-
-    for copy in pin2:
+    for f in range(2):
+        middle(f, 2)
+
+    for copy in pin:
         copy.wait_recv()
     for i in range(piece // 64):
         at = slice(i * 64, (i + 1) * 64)
-        ybuf[0, at, :] = dot(eye[0:64, 0:64], avp[:, at], NT)
-    ybuf[1] = jnp.zeros((piece, lanes), F32)
+        ybuf[at, :] = dot(eye[0:64, 0:64], avp[:, at], NT)
+    ybuf[piece:, :] = jnp.zeros((piece, lanes), F32)
     gram[0] = jnp.zeros((64, lanes), F32)
 
-    def project(b, carry):
-        i, j = lax.div(b, N), lax.rem(b, N)
-        p = pf[j, i]
-        ybuf[0] = ybuf[0] + dot(wbuf[0, b], p, NT)
-        ybuf[1] = ybuf[1] + dot(wbuf[1, b], p, NT)
-        gram[0] = gram[0] + dot(p[0:64], p, NT)
+    def project(j, carry):
+        acc, g = 0.0, 0.0
+        for i in range(N):
+            p = pf[j, i]
+            acc = acc + dot(wbuf[i * N + j], p, NT)
+            g = g + dot(p[0:64], p, NT)
+        ybuf[...] = ybuf[...] + acc
+        gram[0] = gram[0] + g
         return carry
 
-    lax.fori_loop(0, N * N // 2, project, 0)
-    for f in range(2):
-        middle(f, 2)
-    lax.fori_loop(N * N // 2, N * N, project, 0)
-    rload.wait()
-    for s in range(2):
-        for i, part in enumerate(split3(ybuf[s])):
-            yi = part
-            for f in range(2):
-                at = slice(f * half, (f + 1) * half)
-                add = dot(xbuf[s, at, :], yi)
-                if s == 0 and i == 0:
-                    lbuf[at, :] = dot(rbuf[at, :], pf[py, px], NT) + add
-                else:
-                    lbuf[at, :] = lbuf[at, :] + add
+    lax.fori_loop(0, N, project, 0)
+    yx = [
+        send(ybuf.at[pl.ds(s * piece, piece)], yin.at[pl.ds((1 - s) * piece, piece)], c2s.at[33 + s], c2r.at[33 + s], sibling)
+        for s in range(2)
+    ]
+    gin = send(gram.at[0], gram.at[1], c2s.at[1], c2r.at[1], sibling)
     other = pl.multiple_of((1 - core) * half, half)
     mine = pl.multiple_of(core * half, half)
+    rload.wait()
+    lbuf[...] = dot(rbuf[...], pown[...], NT)
     lin = send(lbuf.at[pl.ds(other, half)], la, c2s.at[0], c2r.at[0], sibling)
-    gin = send(gram.at[0], gram.at[1], c2s.at[1], c2r.at[1], sibling)
 
     def stage2(f, c):
         wait_m(f, c, 0, 1)
@@ -318,20 +344,25 @@
             tb[at] = (tb[at].astype(F32) + r2[f, c, direction, 0].astype(F32)).astype(BF16)
             send_n(f, c, direction, 2)
 
-    for f in range(2):
-        stage2(f, 0)
+    for copy in yx:
+        copy.wait_recv()
     lin.wait_recv()
-    lc[...] = lbuf[pl.ds(mine, half), :] + la[...]
+    total = lbuf[pl.ds(mine, half), :] + la[...]
+    for part in split3(ybuf[...] + yin[...]):
+        total = total + dot(xbuf[pl.ds(mine, half), :], part)
+    lc[...] = total
     q = half // (N * N)
 
     def part_of(o):
         return pl.ds(pl.multiple_of((wrap(px + o[0]) * N + wrap(py + o[1])) * q, q), q)
 
     bins = [send(lc.at[part_of(o)], lx.at[i], c2s.at[2 + i], c2r.at[2 + i], away(o)) for i, o in enumerate(same)]
-    for f in range(2):
-        stage2(f, 1)
-    for f in range(2):
-        stage3(f, 0)
+    stage2(0, 0)
+    stage2(1, 0)
+    stage2(0, 1)
+    stage3(0, 0)
+    stage2(1, 1)
+    stage3(1, 0)
     total = lc[part_of((0, 0)), :]
     for i, copy in enumerate(bins):
         copy.wait_recv()
@@ -339,10 +370,10 @@
     lfull[core, px, py] = total
     own = lfull.at[core, px, py]
     dins = [send(own, own, c2s.at[17 + i], c2r.at[17 + i], away(o)) for i, o in enumerate(same)]
-    for f in range(2):
-        stage2(f, 2)
-    for f in range(2):
-        stage3(f, 1)
+    stage2(0, 2)
+    stage3(0, 1)
+    stage2(1, 2)
+    stage3(1, 1)
     for copy in dins:
         copy.wait_recv()
     own = lfull.at[core]
@@ -403,6 +434,9 @@
             ssend[n:n + 1, :] = jnp.sum(sq.T, 0, keepdims=True)
 
     ins = [send(ssend, sx.at[i], c3s.at[i], c3r.at[i], away(o)) for i, o in enumerate(plane)]
+    for copy in sends[:-len(ins)]:
+        copy.wait_send()
+    late = len(sends) - len(ins)
     stot = ssend[...]
     for i, copy in enumerate(ins):
         copy.wait_recv()
@@ -432,7 +466,7 @@
     def fold(m):
         return m[0:n32] + m[n32:2 * n32] + m[2 * n32:3 * n32]
 
-    ggn = fold(dot(uu, xbuf[0]))
+    ggn = fold(dot(uu, xbuf[:, 0:piece]))
     ch = fold(dot(cc, hhi[...]) + dot(cc, hlo[...]))
     curv = SCALE * (dot(jnp.concatenate(t1, 0), g8[...], precision=HI) - ch)
 
@@ -457,7 +491,7 @@
     for copy in ins:
         copy.wait_recv()
     out_ref[...] = zfull[...]
-    for copy in sends:
+    for copy in sends[late:]:
         copy.wait_send()
 
 
@@ -486,20 +520,30 @@
     packed = pl.pallas_call(
         functools.partial(kernel, chunks, zs, rows * zs),
         out_shape=jax.ShapeDtypeStruct((8, 8, 384), F32),
-        in_specs=[hbm, hbm, hbm] + [vmem] * 7,
+        in_specs=[hbm] * 10,
         out_specs=vmem,
         scratch_shapes=[
-            pltpu.VMEM((2, piece, rows), BF16),
-            pltpu.VMEM((2, rows, piece), BF16),
+            pltpu.VMEM(a_in.shape, BF16),
+            pltpu.VMEM(b_out.shape, BF16),
+            pltpu.VMEM(gain.shape, BF16),
+            pltpu.VMEM(head.shape, BF16),
+            pltpu.VMEM((prior.shape[1], rows), F32),
+            pltpu.VMEM((k * rank, piece), BF16),
+            pltpu.VMEM((k * rank, fb), BF16),
+            dma((7,)),
+            pltpu.VMEM((2 * piece, rows), BF16),
+            pltpu.VMEM((rows, 2 * piece), BF16),
             pltpu.VMEM((rows, fb), BF16),
-            pltpu.VMEM((2, N * N, piece, fb), BF16),
+            pltpu.VMEM((N * N, 2 * piece, fb), BF16),
             pltpu.VMEM((2, N * N, 2, half, 128), BF16),
             pltpu.VMEM((2, chunks, 2, 3, 2, 2, tc, 128), BF16),
             pltpu.VMEM((2, chunks, 2, 3, tc, 128), BF16),
             pltpu.VMEM((N, N, 128, fb), BF16),
+            pltpu.VMEM((128, fb), BF16),
             pltpu.VMEM((8, fb), F32),
             pltpu.VMEM((128, piece), BF16),
-            pltpu.VMEM((2, piece, 128), F32),
+            pltpu.VMEM((2 * piece, 128), F32),
+            pltpu.VMEM((2 * piece, 128), F32),
             pltpu.VMEM((2, 64, 128), F32),
             pltpu.VMEM((rows, 128), F32),
             pltpu.VMEM((half, 128), F32),
@@ -517,8 +561,8 @@
             dma((N * N,)), dma((N * N,)), dma((2,)), dma((2,)),
             dma((2, chunks, 2, 3)), dma((2, chunks, 2, 3)),
             dma((2, chunks, 2, 3)), dma((2, chunks, 2, 3)),
-            dma((2, N - 1)), dma((2, N - 1)),
-            dma((33,)), dma((33,)), dma((2 * N * N - 1,)), dma((2 * N * N - 1,)),
+            dma((N * N - 1,)), dma((N * N - 1,)),
+            dma((35,)), dma((35,)), dma((2 * N * N - 1,)), dma((2 * N * N - 1,)),
             dma((2, zs - 1)), dma((2, zs - 1)),
         ],
         compiler_params=pltpu.CompilerParams(

time: 82.9 us -> 79.9 us (0.964)
  Pallas kernels: 82 us -> 78.9 us
    pallas_call x1, Pallas kernels: 80.5 us -> 77.3 us  [shards(): pl.pallas_call(functools.partial(kernel, chunks, zs, rows * zs), out_shap...]
where the time goes in v4:
time: 79.9 us; the launch traced here: 79.5 us
  Pallas kernels  78.9 us (99%)
    pallas_call x1, Pallas kernels, shards(): pl.pallas_call(functools.partial(kernel, chunks, zs, rows * zs), out_shap...  77.3 us

profile of v4, /device:TPU:2, one launch (start us, length us, event | category | flops | bytes accessed | tf_op | source)
XLA Modules:
  0.0 79.5 jit_solution(8249103039270544334)
XLA Ops:
  0.6 77.3 %shard_map.113.in_ref = f32[8,8,384]{2,1,0:T(8,128)} custom-call(bf16[448,768]{1,0:T(8,128)(2,1)} %bitcast.6, bf16[768,256]{1,0:T(8,128)(2,1)} %r_hbm.1, bf16[448,8192]{1,0:T(8,128)(2,1)} %w_hbm.1, bf16[16,448]{1,0:T(8,128)(2,1)} %a_hbm.1, bf16[16,256]{1,0:T(8,128)(2,1)} %b_hbm.1, bf16[256]{0:T(256)(128)(2,1)} %g_hbm.1, bf16[4,256]{1,0:T(4,128)(2,1)} %head_hbm.1, ...), custom_call_target="tpu_custom_call" | custom-call | tf_op jit(solution)/shard_map/pallas_call | solution.py:520
  78.0 1.5 %shard_map.114 = (f32[32,448]{1,0:T(8,128)}, f32[32,256]{1,0:T(8,128)}) custom-call(f32[8,8,384]{2,1,0:T(8,128)} %shard_map.113.in_ref), custom_call_target="tpu_custom_call" | custom-call | tf_op jit(solution)/shard_map/pallas_call | solution.py:575

commit v5 on v4

--- a/solution.py
+++ b/solution.py
@@ -40,7 +40,7 @@
     a_ref, b_ref, g_ref, head_ref, prior_ref, v_ref, d_ref, sl,
     xt, xbuf, rbuf, wbuf, tb, r1, r2, pf, pown, g8, avp, ybuf, yin, gram, lbuf, la, lc, lx, lfull,
     hhi, hlo, ssend, sx, zpart, zrecv, zfull,
-    wl, xl, rl, ws, wr, xs, xr, ms, mr, ns, nr, c1s, c1r, c2s, c2r, c3s, c3r, zss, zsr,
+    wl, xl, rl, ws, wr, xs, xr, ms, mr, ns, nr, c1s, c1r, c2s, c2r, c3s, c3r, zss, zsr, met,
 ):
     piece, rows = x_hbm.shape
     half = rows // 2
@@ -87,12 +87,12 @@
         return copy
 
     barrier = pltpu.get_barrier_semaphore()
-    peers = [away(o) for o in plane] + zpeer[1:]
+    peers = [sibling] + xpeer[1:] + ypeer[1:] + [zpeer[1], zpeer[zs - 1]]
     for to in peers:
         pl.semaphore_signal(barrier, inc=1, device_id=to, device_id_type=pl.DeviceIdType.MESH)
 
     order = [(2, o) for o in range(N)] + [(o, 2) for o in (0, 1, 3)]
-    order += [(i, j) for i in (1, 3, 0) for j in (1, 3, 0)]
+    order += [(i, j) for i in (1, 3, 0) for j in (3, 0, 1)]
 
     def block(n):
         return wrap(px + order[n][0]) * N + wrap(py + order[n][1])
@@ -140,7 +140,8 @@
     avp[64:64 + rank, :] = a_ref[...]
     avp[64 + rank:64 + 3 * rank, :] = v_ref[...]
 
-    pf[py, px, 0:64, :] = pown[0:64, :]
+    share = pl.ds(pl.multiple_of(lax.rem(zi, 2) * 32, 32), 32)
+    pf[py, px, share, :] = pown[share, :]
     pl.semaphore_wait(barrier, len(peers))
 
     def send_x(f):
@@ -152,7 +153,7 @@
     xin = [send_x(0)]
     win = [send_w(n) for n in range(N)]
     pin = [
-        send(pown.at[pl.ds(0, 64)], pf.at[py, px, pl.ds(0, 64)], c1s.at[i], c1r.at[i], away(o)) for i, o in enumerate(same)
+        send(pown.at[share], pf.at[py, px, share], c1s.at[o - 1], c1r.at[o - 1], xpeer[o]) for o in (2, 1, 3)
     ]
     xin.append(send_x(1))
     win += [send_w(n) for n in range(N, N * N)]
@@ -251,24 +252,41 @@
     for n in range(N):
         wait_w(n)
     start(0)
+    for copy in pin:
+        copy.wait_recv()
+    pin = [
+        send(pf.at[py, :, share], pf.at[py, :, share], c1s.at[2 + o], c1r.at[2 + o], ypeer[o]) for o in (2, 1, 3)
+    ]
     first(1)
     for n in range(N, 2 * N - 1):
         wait_w(n)
     start(1)
-    for n in range(2 * N - 1, N * N):
-        wait_w(n)
-
+
+    def greet(n):
+        for to in (zpeer[1], zpeer[zs - 1]):
+            pl.semaphore_signal(met.at[n], inc=1, device_id=to, device_id_type=pl.DeviceIdType.MESH)
+
+    greet(0)
     def send_m2(f, c):
         for direction in range(2):
             send_m(f, c, direction, 1)
 
-    both(4, lambda n: 1 + 2 * lax.div(n, 2), lambda n: 1 + 2 * lax.rem(n, 2))
-    both(2, lambda n: 1 + 2 * n, lambda n: 0)
-    lax.fori_loop(0, 2, single(0, lambda n: 1 + 2 * n), 0)
-    send_m2(0, 0)
-    both(2, lambda n: 0, lambda n: 1 + 2 * n)
-    lax.fori_loop(0, 2, single(1, lambda n: 1 + 2 * n), 0)
-    send_m2(1, 0)
+    for i, o in enumerate((1, 3)):
+        for n in range(2 * N - 1 + 3 * i, 2 * N + 2 + 3 * i):
+            wait_w(n)
+        both(3, lambda n: o, lambda n: N - 1 + n)
+        lax.fori_loop(0, 1, single(0, lambda n: o + n), 0)
+        send_m(0, 0, i, 1)
+    for copy in pin:
+        copy.wait_recv()
+    pair = {"item": zi + 1 - 2 * lax.rem(zi, 2)}
+    pin = [send(pf.at[:, :, share], pf.at[:, :, share], c1s.at[6], c1r.at[6], pair)]
+    for n in range(N * N - 3, N * N):
+        wait_w(n)
+    for i, o in enumerate((1, 3)):
+        both(1, lambda n: n, lambda n: o + n)
+        lax.fori_loop(0, 1, single(1, lambda n: o + n), 0)
+        send_m(1, 0, i, 1)
 
     def middle(f, c):
         for direction in range(2):
@@ -289,6 +307,9 @@
         send_m2(f, 2)
     for f in range(2):
         middle(f, 2)
+
+    pl.semaphore_wait(met.at[0], 2)
+    greet(1)
 
     for copy in pin:
         copy.wait_recv()
@@ -344,6 +365,9 @@
             tb[at] = (tb[at].astype(F32) + r2[f, c, direction, 0].astype(F32)).astype(BF16)
             send_n(f, c, direction, 2)
 
+    pl.semaphore_wait(met.at[1], 2)
+    greet(2)
+
     for copy in yx:
         copy.wait_recv()
     lin.wait_recv()
@@ -360,8 +384,8 @@
     stage2(0, 0)
     stage2(1, 0)
     stage2(0, 1)
+    stage2(1, 1)
     stage3(0, 0)
-    stage2(1, 1)
     stage3(1, 0)
     total = lc[part_of((0, 0)), :]
     for i, copy in enumerate(bins):
@@ -371,8 +395,8 @@
     own = lfull.at[core, px, py]
     dins = [send(own, own, c2s.at[17 + i], c2r.at[17 + i], away(o)) for i, o in enumerate(same)]
     stage2(0, 2)
+    stage2(1, 2)
     stage3(0, 1)
-    stage2(1, 2)
     stage3(1, 1)
     for copy in dins:
         copy.wait_recv()
@@ -380,6 +404,7 @@
     fin = send(own, own, c2s.at[32], c2r.at[32], sibling)
     for f in range(2):
         stage3(f, 2)
+    pl.semaphore_wait(met.at[2], 2)
     fin.wait_recv()
     gin.wait_recv()
 
@@ -561,9 +586,10 @@
             dma((N * N,)), dma((N * N,)), dma((2,)), dma((2,)),
             dma((2, chunks, 2, 3)), dma((2, chunks, 2, 3)),
             dma((2, chunks, 2, 3)), dma((2, chunks, 2, 3)),
-            dma((N * N - 1,)), dma((N * N - 1,)),
+            dma((7,)), dma((7,)),
             dma((35,)), dma((35,)), dma((2 * N * N - 1,)), dma((2 * N * N - 1,)),
             dma((2, zs - 1)), dma((2, zs - 1)),
+            pltpu.SemaphoreType.REGULAR((3,)),
         ],
         compiler_params=pltpu.CompilerParams(
             collective_id=0, has_side_effects=True, vmem_limit_bytes=56 * 1024 * 1024

time: 79.9 us -> 77.7 us (0.972)
  Pallas kernels: 78.9 us -> 76.9 us
    pallas_call x1, Pallas kernels: 77.3 us -> 75.4 us  [shards(): pl.pallas_call(functools.partial(kernel, chunks, zs, rows * zs), out_shap...]
where the time goes in v5:
time: 77.7 us; the launch traced here: 77.6 us
  Pallas kernels  76.9 us (99%)
    pallas_call x1, Pallas kernels, shards(): pl.pallas_call(functools.partial(kernel, chunks, zs, rows * zs), out_shap...  75.4 us

profile of v5, /device:TPU:2, one launch (start us, length us, event | category | flops | bytes accessed | tf_op | source)
XLA Modules:
  0.0 77.6 jit_solution(4244391587590848249)
XLA Ops:
  0.6 75.4 %shard_map.113.in_ref = f32[8,8,384]{2,1,0:T(8,128)} custom-call(bf16[448,768]{1,0:T(8,128)(2,1)} %bitcast.6, bf16[768,256]{1,0:T(8,128)(2,1)} %r_hbm.1, bf16[448,8192]{1,0:T(8,128)(2,1)} %w_hbm.1, bf16[16,448]{1,0:T(8,128)(2,1)} %a_hbm.1, bf16[16,256]{1,0:T(8,128)(2,1)} %b_hbm.1, bf16[256]{0:T(256)(128)(2,1)} %g_hbm.1, bf16[4,256]{1,0:T(4,128)(2,1)} %head_hbm.1, ...), custom_call_target="tpu_custom_call" | custom-call | tf_op jit(solution)/shard_map/pallas_call | solution.py:545
  76.0 1.5 %shard_map.114 = (f32[32,448]{1,0:T(8,128)}, f32[32,256]{1,0:T(8,128)}) custom-call(f32[8,8,384]{2,1,0:T(8,128)} %shard_map.113.in_ref), custom_call_target="tpu_custom_call" | custom-call | tf_op jit(solution)/shard_map/pallas_call | solution.py:601

commit v6 on v5

--- a/solution.py
+++ b/solution.py
@@ -75,6 +75,13 @@
     def away(o):
         return device(wrap(px + o[0]), wrap(py + o[1]), lax.rem(core + o[2], 2))
 
+    pa, pb = px + core * (py - px), py + core * (px - py)
+    apeer = [None] + [device(wrap(px + o * (1 - core)), wrap(py + o * core), core) for o in range(1, N)]
+    bpeer = [None] + [device(wrap(px + o * core), wrap(py + o * (1 - core)), core) for o in range(1, N)]
+
+    def index(i, j, c):
+        return i * (N - (N - 1) * c) + j * (1 + (N - 1) * c)
+
     sends = []
 
     def send(src, dst, ssem, rsem, to):
@@ -95,7 +102,14 @@
     order += [(i, j) for i in (1, 3, 0) for j in (3, 0, 1)]
 
     def block(n):
-        return wrap(px + order[n][0]) * N + wrap(py + order[n][1])
+        if n < N:
+            return index(wrap(pa + 2), n, core)
+        return index(wrap(pa + order[n][0]), wrap(pb + order[n][1]), core)
+
+    def other_block(n):
+        if n < N:
+            return index(wrap(pb + 2), n, 1 - core)
+        return index(wrap(pb + order[n][0]), wrap(pa + order[n][1]), 1 - core)
 
     def columns(b, c):
         return pl.ds(pl.multiple_of((b * 2 + c) * fb, fb), fb)
@@ -141,19 +155,19 @@
     avp[64 + rank:64 + 3 * rank, :] = v_ref[...]
 
     share = pl.ds(pl.multiple_of(lax.rem(zi, 2) * 32, 32), 32)
-    pf[py, px, share, :] = pown[share, :]
+    pf[pb, pa, share, :] = pown[share, :]
     pl.semaphore_wait(barrier, len(peers))
 
     def send_x(f):
         return send(x_hbm.at[:, pl.ds(f * half, half)], xt.at[pl.ds(piece, piece), pl.ds(f * half, half)], xs.at[f], xr.at[f], sibling)
 
     def send_w(n):
-        return send(w_hbm.at[:, columns(block(n), 1 - core)], wbuf.at[block(n), pl.ds(piece, piece)], ws.at[n], wr.at[n], sibling)
+        return send(w_hbm.at[:, columns(other_block(n), 1 - core)], wbuf.at[other_block(n), pl.ds(piece, piece)], ws.at[n], wr.at[n], sibling)
 
     xin = [send_x(0)]
     win = [send_w(n) for n in range(N)]
     pin = [
-        send(pown.at[share], pf.at[py, px, share], c1s.at[o - 1], c1r.at[o - 1], xpeer[o]) for o in (2, 1, 3)
+        send(pown.at[share], pf.at[pb, pa, share], c1s.at[o - 1], c1r.at[o - 1], apeer[o]) for o in (2, 1, 3)
     ]
     xin.append(send_x(1))
     win += [send_w(n) for n in range(N, N * N)]
@@ -161,7 +175,7 @@
     def recv_slot(src_shape_ref, sem):
         return pltpu.make_async_copy(src_shape_ref, src_shape_ref, sem)
 
-    pos = [(px, py), (py, px)]
+    pos = [(pa, pb), (pb, pa)]
 
     eye = (
         lax.broadcasted_iota(jnp.int32, (lanes, lanes), 0) == lax.broadcasted_iota(jnp.int32, (lanes, lanes), 1)
@@ -178,7 +192,7 @@
 
     def group(f, i1, lo=0, hi=N):
         def body(i2, carry):
-            b = i1 * N + i2 if f == 0 else i2 * N + i1
+            b = index(i1, i2, core) if f == 0 else index(i2, i1, core)
             put(f, i1, i2, dot(xbuf[f * half:(f + 1) * half, :], wbuf[b]).astype(BF16))
             return carry
 
@@ -186,8 +200,8 @@
 
     def both(count, ox, oy):
         def body(n, carry):
-            x, y = wrap(px + ox(n)), wrap(py + oy(n))
-            out = dot(xbuf[...], wbuf[x * N + y]).astype(BF16)
+            x, y = wrap(pa + ox(n)), wrap(pb + oy(n))
+            out = dot(xbuf[...], wbuf[index(x, y, core)]).astype(BF16)
             put(0, x, y, out[:half])
             put(1, y, x, out[half:])
             return carry
@@ -197,14 +211,14 @@
     def single(f, offsets):
         def body(n, carry):
             i1, i2 = wrap(pos[f][0] + offsets(n)), wrap(pos[f][1] + 2)
-            b = i1 * N + i2 if f == 0 else i2 * N + i1
+            b = index(i1, i2, core) if f == 0 else index(i2, i1, core)
             put(f, i1, i2, dot(xbuf[f * half:(f + 1) * half, :], wbuf[b]).astype(BF16))
             return carry
 
         return body
 
     def send_m(f, c, direction, msg):
-        peer = xpeer if f == 0 else ypeer
+        peer = apeer if f == 0 else bpeer
         to = peer[1] if direction == 0 else peer[N - 1]
         offset = 2 if msg == 0 else (1 if direction == 0 else N - 1)
         i1 = wrap(pos[f][0] + offset)
@@ -219,7 +233,7 @@
         recv_slot(r1.at[f, c, direction, msg], mr.at[f, c, direction, msg]).wait()
 
     def send_n(f, c, direction, msg):
-        peer = ypeer if f == 0 else xpeer
+        peer = bpeer if f == 0 else apeer
         to = peer[1] if direction == 0 else peer[N - 1]
         offset = 2 if msg == 0 else (1 if direction == 0 else N - 1)
         i2 = wrap(pos[f][1] + offset)
@@ -235,7 +249,7 @@
 
     def wait_w(n):
         wloads[n].wait()
-        win[n].wait_recv()
+        recv_slot(wbuf.at[block(n), pl.ds(piece, piece)], wr.at[n]).wait()
 
     def first(f):
         xloads[f].wait()
@@ -244,18 +258,19 @@
 
     def start(f):
         for direction in range(2):
+            if f == 0:
+                wait_w(2 * direction)
+                wait_w(2 * direction + 1)
             group(f, wrap(pos[f][0] + 2), 2 * direction, 2 * direction + 2)
             for c in range(chunks):
                 send_m(f, c, direction, 0)
 
     first(0)
-    for n in range(N):
-        wait_w(n)
     start(0)
     for copy in pin:
         copy.wait_recv()
     pin = [
-        send(pf.at[py, :, share], pf.at[py, :, share], c1s.at[2 + o], c1r.at[2 + o], ypeer[o]) for o in (2, 1, 3)
+        send(pf.at[pb, :, share], pf.at[pb, :, share], c1s.at[2 + o], c1r.at[2 + o], bpeer[o]) for o in (2, 1, 3)
     ]
     first(1)
     for n in range(N, 2 * N - 1):
@@ -323,7 +338,7 @@
         acc, g = 0.0, 0.0
         for i in range(N):
             p = pf[j, i]
-            acc = acc + dot(wbuf[i * N + j], p, NT)
+            acc = acc + dot(wbuf[index(i, j, core)], p, NT)
             g = g + dot(p[0:64], p, NT)
         ybuf[...] = ybuf[...] + acc
         gram[0] = gram[0] + g
@@ -385,8 +400,6 @@
     stage2(1, 0)
     stage2(0, 1)
     stage2(1, 1)
-    stage3(0, 0)
-    stage3(1, 0)
     total = lc[part_of((0, 0)), :]
     for i, copy in enumerate(bins):
         copy.wait_recv()
@@ -394,6 +407,8 @@
     lfull[core, px, py] = total
     own = lfull.at[core, px, py]
     dins = [send(own, own, c2s.at[17 + i], c2r.at[17 + i], away(o)) for i, o in enumerate(same)]
+    stage3(0, 0)
+    stage3(1, 0)
     stage2(0, 2)
     stage2(1, 2)
     stage3(0, 1)

time: 77.7 us -> 76.1 us (0.979)
  Pallas kernels: 76.9 us -> 75.2 us
    pallas_call x1, Pallas kernels: 75.4 us -> 73.7 us  [shards(): pl.pallas_call(functools.partial(kernel, chunks, zs, rows * zs), out_shap...]
where the time goes in v6:
time: 76.1 us; the launch traced here: 75.9 us
  Pallas kernels  75.2 us (99%)
    pallas_call x1, Pallas kernels, shards(): pl.pallas_call(functools.partial(kernel, chunks, zs, rows * zs), out_shap...  73.7 us
    pallas_call x1, Pallas kernels, shards(): pl.pallas_call(unpack, out_shape=(jax.ShapeDtypeStruct((k * rank, piece),...  1.54 us

profile of v6, /device:TPU:2, one launch (start us, length us, event | category | flops | bytes accessed | tf_op | source)
XLA Modules:
  0.0 75.9 jit_solution(622052309424233062)
XLA Ops:
  0.6 73.7 %shard_map.113.in_ref = f32[8,8,384]{2,1,0:T(8,128)} custom-call(bf16[448,768]{1,0:T(8,128)(2,1)} %bitcast.6, bf16[768,256]{1,0:T(8,128)(2,1)} %r_hbm.1, bf16[448,8192]{1,0:T(8,128)(2,1)} %w_hbm.1, bf16[16,448]{1,0:T(8,128)(2,1)} %a_hbm.1, bf16[16,256]{1,0:T(8,128)(2,1)} %b_hbm.1, bf16[256]{0:T(256)(128)(2,1)} %g_hbm.1, bf16[4,256]{1,0:T(4,128)(2,1)} %head_hbm.1, ...), custom_call_target="tpu_custom_call" | custom-call | tf_op jit(solution)/shard_map/pallas_call | solution.py:560
  74.4 1.5 %shard_map.114 = (f32[32,448]{1,0:T(8,128)}, f32[32,256]{1,0:T(8,128)}) custom-call(f32[8,8,384]{2,1,0:T(8,128)} %shard_map.113.in_ref), custom_call_target="tpu_custom_call" | custom-call | tf_op jit(solution)/shard_map/pallas_call | solution.py:616

commit v7 on v6

--- a/solution.py
+++ b/solution.py
@@ -292,10 +292,12 @@
         both(3, lambda n: o, lambda n: N - 1 + n)
         lax.fori_loop(0, 1, single(0, lambda n: o + n), 0)
         send_m(0, 0, i, 1)
-    for copy in pin:
-        copy.wait_recv()
-    pair = {"item": zi + 1 - 2 * lax.rem(zi, 2)}
-    pin = [send(pf.at[:, :, share], pf.at[:, :, share], c1s.at[6], c1r.at[6], pair)]
+        if i == 0:
+            for copy in pin:
+                copy.wait_recv()
+            pair = {"item": zi + 1 - 2 * lax.rem(zi, 2)}
+            for j in range(N):
+                send(pf.at[j, :, share], pf.at[j, :, share], c1s.at[6 + j], c1r.at[6 + j], pair)
     for n in range(N * N - 3, N * N):
         wait_w(n)
     for i, o in enumerate((1, 3)):
@@ -320,14 +322,11 @@
     for f in range(2):
         middle(f, 1)
         send_m2(f, 2)
-    for f in range(2):
-        middle(f, 2)
 
     pl.semaphore_wait(met.at[0], 2)
     greet(1)
 
-    for copy in pin:
-        copy.wait_recv()
+    theirs = pl.ds(pl.multiple_of((1 - lax.rem(zi, 2)) * 32, 32), 32)
     for i in range(piece // 64):
         at = slice(i * 64, (i + 1) * 64)
         ybuf[at, :] = dot(eye[0:64, 0:64], avp[:, at], NT)
@@ -336,6 +335,7 @@
 
     def project(j, carry):
         acc, g = 0.0, 0.0
+        recv_slot(pf.at[j, :, theirs], c1r.at[6 + j]).wait()
         for i in range(N):
             p = pf[j, i]
             acc = acc + dot(wbuf[index(i, j, core)], p, NT)
@@ -350,6 +350,8 @@
         for s in range(2)
     ]
     gin = send(gram.at[0], gram.at[1], c2s.at[1], c2r.at[1], sibling)
+    for f in range(2):
+        middle(f, 2)
     other = pl.multiple_of((1 - core) * half, half)
     mine = pl.multiple_of(core * half, half)
     rload.wait()
@@ -413,12 +415,12 @@
     stage2(1, 2)
     stage3(0, 1)
     stage3(1, 1)
+    stage3(0, 2)
     for copy in dins:
         copy.wait_recv()
     own = lfull.at[core]
     fin = send(own, own, c2s.at[32], c2r.at[32], sibling)
-    for f in range(2):
-        stage3(f, 2)
+    stage3(1, 2)
     pl.semaphore_wait(met.at[2], 2)
     fin.wait_recv()
     gin.wait_recv()
@@ -601,7 +603,7 @@
             dma((N * N,)), dma((N * N,)), dma((2,)), dma((2,)),
             dma((2, chunks, 2, 3)), dma((2, chunks, 2, 3)),
             dma((2, chunks, 2, 3)), dma((2, chunks, 2, 3)),
-            dma((7,)), dma((7,)),
+            dma((10,)), dma((10,)),
             dma((35,)), dma((35,)), dma((2 * N * N - 1,)), dma((2 * N * N - 1,)),
             dma((2, zs - 1)), dma((2, zs - 1)),
             pltpu.SemaphoreType.REGULAR((3,)),

time: 76.1 us -> 76 us (level)
  no operation moved by 1% of the time
where the time goes in v7:
time: 76 us; the launch traced here: 75.9 us
  Pallas kernels  75.3 us (99%)
    pallas_call x1, Pallas kernels, shards(): pl.pallas_call(functools.partial(kernel, chunks, zs, rows * zs), out_shap...  73.7 us
    pallas_call x1, Pallas kernels, shards(): pl.pallas_call(unpack, out_shape=(jax.ShapeDtypeStruct((k * rank, piece),...  1.54 us

profile of v7, /device:TPU:2, one launch (start us, length us, event | category | flops | bytes accessed | tf_op | source)
XLA Modules:
  0.0 75.9 jit_solution(16439364221736876696)
XLA Ops:
  0.6 73.7 %shard_map.113.in_ref = f32[8,8,384]{2,1,0:T(8,128)} custom-call(bf16[448,768]{1,0:T(8,128)(2,1)} %bitcast.6, bf16[768,256]{1,0:T(8,128)(2,1)} %r_hbm.1, bf16[448,8192]{1,0:T(8,128)(2,1)} %w_hbm.1, bf16[16,448]{1,0:T(8,128)(2,1)} %a_hbm.1, bf16[16,256]{1,0:T(8,128)(2,1)} %b_hbm.1, bf16[256]{0:T(256)(128)(2,1)} %g_hbm.1, bf16[4,256]{1,0:T(4,128)(2,1)} %head_hbm.1, ...), custom_call_target="tpu_custom_call" | custom-call | tf_op jit(solution)/shard_map/pallas_call | solution.py:562
  74.4 1.5 %shard_map.114 = (f32[32,448]{1,0:T(8,128)}, f32[32,256]{1,0:T(8,128)}) custom-call(f32[8,8,384]{2,1,0:T(8,128)} %shard_map.113.in_ref), custom_call_target="tpu_custom_call" | custom-call | tf_op jit(solution)/shard_map/pallas_call | solution.py:618
